TPU v7x, 32 devices: a whole 2x2x4 slice. The times are simulated.
32 devices in a mesh: band: 16 (over z, x, core), batch: 2 (over y).
Axes of the slice: x: 2, y: 2, z: 4, core: 2. Of those that a mesh axis runs over, the one named last changes fastest.
Arguments:
- incoming_rows: bfloat16 [2, 16384, 512], P('batch', 'band'), may hold values from -6 to 6
- picture_label: int32 [2, 16384], P('batch', 'band'), may hold values from -1 to 12, as said below
- triple_kernel: float32 [512, 1536], P(('band', 'batch')), may hold values from -0.25 to 0.25
- mixer_kernel: float32 [512, 512], P(('band', 'batch')), may hold values from -2 to 2
- widening_kernel: float32 [512, 2048], P(('band', 'batch')), may hold values from -0.25 to 0.25
- narrowing_kernel: float32 [2048, 512], P(('band', 'batch')), may hold values from -0.125 to 0.125
- asker_offset: float32 [512], P(('band', 'batch')), may hold values from -3 to 3
- content_offset: float32 [512], P(('band', 'batch')), may hold values from -3 to 3
- mixer_offset_vector: float32 [512], P(('band', 'batch')), may hold values from -3 to 3
- widening_offset: float32 [2048], P(('band', 'batch')), may hold values from -3 to 3
- narrowing_offset: float32 [512], P(('band', 'batch')), may hold values from -3 to 3
- leading_gain: float32 [512], P(('band', 'batch')), may hold values from 0.5 to 2
- leading_offset: float32 [512], P(('band', 'batch')), may hold values from -2 to 2
- second_gain: float32 [512], P(('band', 'batch')), may hold values from 0.5 to 2
- second_offset: float32 [512], P(('band', 'batch')), may hold values from -2 to 2
- loss_sensitivity: bfloat16 [2, 16384, 512], P('batch', 'band'), may hold values from -6 to 6
Outputs:
- layer_out: bfloat16 [2, 16384, 512], P('batch', 'band')
- input_grad: bfloat16 [2, 16384, 512], P('batch', 'band')
- qkv_grad: float32 [512, 1536], P(('band', 'batch'))
- proj_grad: float32 [512, 512], P(('band', 'batch'))
- expand_grad: float32 [512, 2048], P(('band', 'batch'))
- reduce_grad: float32 [2048, 512], P(('band', 'batch'))
- query_grad: float32 [512], P(('band', 'batch'))
- value_grad: float32 [512], P(('band', 'batch'))
- attn_grad: float32 [512], P(('band', 'batch'))
- hidden_grad: float32 [2048], P(('band', 'batch'))
- mlp_grad: float32 [512], P(('band', 'batch'))
- prescale_grad: float32 [512], P(('band', 'batch'))
- preshift_grad: float32 [512], P(('band', 'batch'))
- midscale_grad: float32 [512], P(('band', 'batch'))
- midshift_grad: float32 [512], P(('band', 'batch'))
Inputs may be any that keep to these rules, and one draw needn't show every extreme that they name: `picture_label`: in every group the first 256 rows of each band of 1024 rows belong to image 0; the rest of a band holds its thumbnails numbered 1, 2, ... in order, 64 rows each, then padding rows marked -1. Thumbnail numbers count within a band only. Every group has a band filled with thumbnails and a band with a single thumbnail.
All inputs are finite; a program needn't handle non-finite values.
Results may differ from a plain program's by a relative error of at most 0.018.
Values may be sent and summed in bfloat16 or wider, within the bound.
No kernel may reach another device: no remote copies, remote signals or barrier semaphores. Data moves between devices by JAX's collectives and lax.ppermute only.
A program may use at most 256 MiB of HBM per device.

v0:
```python
import functools
import math

import jax
import jax.numpy as jnp
from jax import lax
from jax.experimental import pallas as pl
from jax.experimental.pallas import tpu as pltpu
from jax.sharding import PartitionSpec as P

HEADS = 8
HEAD = 64
LONG = 256
WIDTH = 512
FF = 2048
GROUP = 256
TILE = 512
epsilon = 1e-06
gelu_scale = 0.7978845608028654
f32 = jnp.float32
bf16 = jnp.bfloat16
PARAMS = dict(vmem_limit_bytes=58 << 20)


def dot(left, right, cl=1, cr=0):
    return lax.dot_general(left, right, (((cl,), (cr,)), ((), ())), preferred_element_type=f32)


def standardize(rows):
    center = rows - jnp.mean(rows, axis=1, keepdims=True)
    inverse = lax.rsqrt(jnp.mean(center * center, axis=1, keepdims=True) + epsilon)
    return center * inverse, inverse


def norm_backward(incoming, standard, inverse, scaling):
    scaled = incoming * scaling
    return inverse * (
        scaled
        - jnp.mean(scaled, axis=1, keepdims=True)
        - standard * jnp.mean(scaled * standard, axis=1, keepdims=True)
    )


def column_sum(rows):
    return jnp.sum(rows, axis=0, keepdims=True)


def head_lanes(block, head):
    lane = lax.broadcasted_iota(jnp.int32, block.shape, 1) // HEAD
    return jnp.where(lane == head, block.astype(f32), 0.0).astype(bf16)


V_ASK, V_CONTENT, V_MIXER, V_NARROW, V_G1, V_O1, V_G2, V_O2 = range(8)


def row_of(table_ref, index):
    return table_ref[index : index + 1, :]


def whole(shape):
    return pl.BlockSpec(shape, lambda *_: (0,) * len(shape))


def once(shape):
    return pl.BlockSpec(shape, lambda *_: (0,) * len(shape), pipeline_mode=pl.Buffered(1))


ANYWHERE = pl.BlockSpec(memory_space=pl.ANY)


def behind(kernel, count, prefetch=True):
    skip = 1 if prefetch else 0
    return lambda *refs: kernel(*refs[:skip], *refs[skip + count :])


SIDE = 128
FIRST = 3 * WIDTH + SIDE
SECOND = WIDTH + 2 * FF


class Layout:
    def __init__(self, bands, batches):
        self.bands, self.batches = bands, batches
        self.depth = bands // 4
        self.shards = bands * batches
        self.rows = WIDTH // self.shards
        self.pieces = self.rows % 16 == 0
        self.plane = [(kx, ky) for kx in (0, 1) for ky in range(batches)]

    def shard(self, place, kc, kx, ky, kz, sign):
        z = lax.rem(place[2] + (self.depth + sign * kz), self.depth)
        x = lax.rem(place[3] + kx, 2)
        y = lax.rem(place[4] + (self.batches + sign * ky), self.batches)
        core = lax.rem(place[1] + kc, 2)
        return ((z * 2 + x) * 2 + core) * self.batches + y

    def chip(self, place, kx, kz):
        return lax.rem(place[2] + kz, self.depth) * 2 + lax.rem(place[3] + kx, 2)

    def shift_depth(self, block, k):
        pairs = [(i, ((i // 4 + k) % self.depth) * 4 + i % 4) for i in range(self.bands)]
        return lax.ppermute(block, "band", pairs)

    def flip(self, block, bit):
        return lax.ppermute(block, "band", [(i, i ^ bit) for i in range(self.bands)])

    def shift_plane(self, block, kx, ky):
        n = self.batches
        pairs = [
            (b * n + y, (b ^ (2 * kx)) * n + (y + ky) % n) for b in range(self.bands) for y in range(n)
        ]
        return lax.ppermute(block, ("band", "batch"), pairs)

    def gather_depth(self, block, deps=()):
        return stack_blocks([block] + [self.shift_depth(block, k) for k in range(1, self.depth)], deps)

    def gather_plane(self, stack):
        return [stack if k == (0, 0) else self.shift_plane(stack, *k) for k in self.plane]

    def gather_core(self, plane):
        return plane + [self.flip(part, 1) for part in plane]

    def gather_whole(self, block):
        return [lax.all_gather(block, ("band", "batch"), axis=0, tiled=True)]

    def gathered_specs(self, columns):
        if not self.pieces:
            return [once((WIDTH, columns))]
        return [once((self.depth, self.rows, columns))] * (2 * len(self.plane))

    def each_gathered(self, place, refs, visit):
        if not self.pieces:
            for low in range(0, WIDTH, 16):
                visit(low // 16, refs[0][low : low + 16, :])
            return
        index = 0
        for kc in (0, 1):
            for kx, ky in self.plane:
                for kz in range(self.depth):
                    visit(self.shard(place, kc, kx, ky, kz, -1), refs[index][kz])
                index += 1

    def scattered_shapes(self, columns):
        if not self.pieces:
            return [jax.ShapeDtypeStruct((WIDTH, columns), bf16)]
        shape = (len(self.plane), self.depth, self.rows, columns)
        return [jax.ShapeDtypeStruct(shape, bf16)] * 2

    def store_scattered(self, place, refs, take):
        if not self.pieces:
            for low in range(0, WIDTH, 16):
                refs[0][low : low + 16, :] = take(low // 16)
            return
        for kc in (0, 1):
            for n, (kx, ky) in enumerate(self.plane):
                for kz in range(self.depth):
                    refs[kc][n, kz] = take(self.shard(place, kc, kx, ky, kz, 1))

    def scatter_core(self, parts):
        keep, send = parts
        arrived = self.flip(send, 1)
        return [(keep[n].astype(f32) + arrived[n].astype(f32)).astype(bf16) for n in range(len(self.plane))]

    def scatter_plane(self, pairs):
        arrived = [self.shift_plane(pairs[n], *k) for n, k in enumerate(self.plane) if n]
        return self.add_depth(pairs[:1] + arrived)

    def add_depth(self, stacks):
        totals = []
        for k in range(self.depth):
            total = stacks[0][k].astype(f32)
            for stack in stacks[1:]:
                total = total + stack[k].astype(f32)
            totals.append(total if k == 0 else total.astype(bf16))
        return totals

    def scatter_depth(self, totals, sign=1):
        final = totals[0]
        for k in range(1, self.depth):
            final = final + self.shift_depth(totals[k], (sign * k) % self.depth).astype(f32)
        return final

    def scatter_whole(self, part):
        return lax.psum_scatter(part, ("band", "batch"), scatter_dimension=0, tiled=True).astype(f32)


def tie(values, deps):
    count = len(values)
    return pl.pallas_call(
        lambda *refs: None,
        in_specs=[ANYWHERE] * (count + len(deps)),
        out_specs=[ANYWHERE] * count,
        out_shape=[jax.ShapeDtypeStruct(v.shape, v.dtype) for v in values],
        input_output_aliases={i: i for i in range(count)},
        name="tie",
    )(*values, *deps)


def stack_kernel(*refs):
    for index, ref in enumerate(refs[:-1]):
        refs[-1][index] = ref[...]


def stack_blocks(blocks, deps):
    shape = blocks[0].shape
    return pl.pallas_call(
        behind(stack_kernel, len(deps), False),
        in_specs=[ANYWHERE] * len(deps) + [pl.BlockSpec(memory_space=pltpu.VMEM)] * len(blocks),
        out_shape=jax.ShapeDtypeStruct((len(blocks), *shape), blocks[0].dtype),
        name="stack_blocks",
    )(*deps, *blocks)


def pack_first_kernel(triple_ref, *refs):
    vectors, wide, out_ref, table = refs[:8], *refs[8:]
    shard = triple_ref.shape[0]
    table[...] = jnp.zeros_like(table)
    for index, ref in enumerate(vectors):
        table[index : index + 1, :shard] = ref[...]
    out_ref[:, : 3 * WIDTH] = triple_ref[...].astype(bf16)
    turned = table[...].T[:shard, :]
    across = jnp.pad(wide[...], ((0, shard - 1), (SIDE - 4 * shard, 0)))
    out_ref[:, 3 * WIDTH :] = (turned + across).astype(bf16)


def pack_first(triple, vectors, wide):
    shard = triple.shape[0]
    return pl.pallas_call(
        pack_first_kernel,
        out_shape=jax.ShapeDtypeStruct((shard, FIRST), bf16),
        scratch_shapes=[pltpu.VMEM((SIDE, SIDE), f32)],
        compiler_params=pltpu.CompilerParams(**PARAMS),
        name="pack_first",
    )(triple, *[v[None, :] for v in vectors], wide[None, :])


def pack_rows_kernel(rows_ref, out_ref):
    out_ref[...] = rows_ref[...]


def pack_rows(rows, deps):
    block = pl.BlockSpec((LONG, WIDTH), lambda i: (0, 0))
    return pl.pallas_call(
        behind(pack_rows_kernel, len(deps), False),
        grid=(1,),
        in_specs=[ANYWHERE] * len(deps) + [block],
        out_specs=block,
        out_shape=jax.ShapeDtypeStruct((LONG, WIDTH), bf16),
        name="pack_rows",
    )(*deps, rows)


def pack_second_kernel(mixer_ref, widening_ref, narrowing_ref, out_ref):
    shard = mixer_ref.shape[0]
    out_ref[:, :WIDTH] = mixer_ref[...].astype(bf16)
    out_ref[:, WIDTH : WIDTH + FF] = widening_ref[...].astype(bf16)
    for k in range(4):
        low = WIDTH + FF + k * WIDTH
        out_ref[:, low : low + WIDTH] = narrowing_ref[k * shard : (k + 1) * shard, :].astype(bf16)


def pack_second(mixer, widening, narrowing, deps):
    blocks = [pl.BlockSpec(memory_space=pltpu.VMEM)] * 3
    return pl.pallas_call(
        behind(pack_second_kernel, len(deps), False),
        out_shape=jax.ShapeDtypeStruct((mixer.shape[0], SECOND), bf16),
        in_specs=[ANYWHERE] * len(deps) + blocks,
        compiler_params=pltpu.CompilerParams(**PARAMS),
        name="pack_second",
    )(*deps, mixer, widening, narrowing)


def short_qkv_kernel(layout, place_ref, x_ref, *refs):
    count = len(layout.gathered_specs(FIRST))
    pieces = refs[:count]
    n1_ref, q_ref, k_ref, v_ref, kt_ref, vt_ref, w_ref, vec_ref, hid_ref, side, spread = refs[count:]

    @pl.when(pl.program_id(0) == 0)
    def _():
        def visit(block, rows):
            span = pl.ds(pl.multiple_of(block * 16, 16), 16)
            w_ref[span, :] = rows[:, : 3 * WIDTH]
            side[span, :] = rows[:, 3 * WIDTH :].astype(f32)
            if layout.pieces:
                spread[pl.ds(block, 1), :] = rows[0:1, 3 * WIDTH :].astype(f32)

        layout.each_gathered(place_ref, pieces, visit)
        vec_ref[...] = side[...].T[:16, :]
        if layout.pieces:
            shard = 4 * layout.rows
            for index in range(layout.shards):
                hid_ref[:, index * shard : (index + 1) * shard] = spread[index : index + 1, SIDE - shard :]

    standard, _ = standardize(x_ref[...].astype(f32))
    normed = (standard * row_of(vec_ref, V_G1) + row_of(vec_ref, V_O1)).astype(bf16)
    n1_ref[...] = normed
    projected = dot(normed, w_ref[...])
    q = (projected[:, :WIDTH] + row_of(vec_ref, V_ASK)).astype(bf16)
    q_ref[...] = (q.astype(f32) * (1.0 / math.sqrt(HEAD))).astype(bf16)
    k = projected[:, WIDTH : 2 * WIDTH]
    v = projected[:, 2 * WIDTH :] + row_of(vec_ref, V_CONTENT)
    k_ref[...] = k.astype(bf16)
    v_ref[...] = v.astype(bf16)
    kt_ref[...] = k.T.astype(bf16)
    vt_ref[...] = v.T.astype(bf16)


def short_qkv(layout, place, rows, pieces):
    count = rows.shape[0] - LONG
    block = 256
    row_spec = pl.BlockSpec((block, WIDTH), lambda i, _: (i, 0))
    col_spec = pl.BlockSpec((WIDTH, block), lambda i, _: (0, i))
    flat = jax.ShapeDtypeStruct((count, WIDTH), bf16)
    tall = jax.ShapeDtypeStruct((WIDTH, count), bf16)
    return pl.pallas_call(
        functools.partial(short_qkv_kernel, layout),
        grid_spec=pltpu.PrefetchScalarGridSpec(
            num_scalar_prefetch=1,
            grid=(count // block,),
            in_specs=[pl.BlockSpec((block, WIDTH), lambda i, _: (i + LONG // block, 0))]
            + layout.gathered_specs(FIRST),
            out_specs=[row_spec, row_spec, row_spec, row_spec, col_spec, col_spec]
            + [once((WIDTH, 3 * WIDTH)), whole((16, WIDTH)), whole((1, FF))],
            scratch_shapes=[pltpu.VMEM((WIDTH, SIDE), f32), pltpu.VMEM((max(8, layout.shards), SIDE), f32)],
        ),
        out_shape=[flat, flat, flat, flat, tall, tall]
        + [
            jax.ShapeDtypeStruct((WIDTH, 3 * WIDTH), bf16),
            jax.ShapeDtypeStruct((16, WIDTH), f32),
            jax.ShapeDtypeStruct((1, FF), f32),
        ],
        compiler_params=pltpu.CompilerParams(**PARAMS),
        cost_estimate=pl.CostEstimate(
            flops=2 * count * WIDTH * 3 * WIDTH, bytes_accessed=10 << 20, transcendentals=0
        ),
        name="short_qkv",
    )(place, rows, *pieces)


def short_forward_kernel(
    q_ref, k_ref, vt_ref, idc_ref, idr_ref, e_ref, o_ref, linv_ref, att_ref, s_ref, bias_ref, top_ref
):
    step = pl.program_id(0)
    count = k_ref.shape[0]
    tile = count

    @pl.when(step == 0)
    def _():
        same = idc_ref[...] == idr_ref[...]
        bias_ref[...] = jnp.where(same, 0.0, -1e30)

    def first(slot):
        masked = head_lanes(q_ref[...], lax.rem(step, 4))
        top = None
        for low in range(0, count, tile):
            s = dot(k_ref[low : low + tile, :], masked, 1, 1) + bias_ref[low : low + tile, :]
            s_ref[slot, low : low + tile, :] = s
            part = jnp.max(s, axis=0, keepdims=True)
            top = part if top is None else jnp.maximum(top, part)
        top_ref[slot] = jnp.broadcast_to(top, (8, count))

    def second(slot):
        head = step - 1
        top = top_ref[slot, 0:1, :]
        mixed = jnp.zeros((HEAD, count), f32)
        total = jnp.zeros((1, count), f32)
        for low in range(0, count, tile):
            e = jnp.exp(s_ref[slot, low : low + tile, :] - top)
            total += column_sum(e)
            low_e = e.astype(bf16)
            e_ref[low : low + tile, :] = low_e
            mixed += dot(vt_ref[pl.ds(pl.multiple_of(head * HEAD, HEAD), HEAD), low : low + tile], low_e)
        linv = 1.0 / total
        linv_ref[...] = jnp.broadcast_to(linv, (8, count))
        o_ref[pl.ds(pl.multiple_of(head * HEAD, HEAD), HEAD), :] = mixed * linv

    last = pl.num_programs(0) - 1

    @pl.when(step == 0)
    def _():
        first(0)

    for parity in (0, 1):
        @pl.when((step > 0) & (step < last) & (lax.rem(step, 2) == parity))
        def _():
            first(parity)
            second(1 - parity)

    @pl.when(step == last)
    def _():
        second((HEADS - 1) % 2)
        for low in range(0, WIDTH, 128):
            att_ref[:, low : low + 128] = o_ref[low : low + 128, :].T.astype(bf16)


def short_forward(q, k, vt, ids, deps):
    count = q.shape[0]
    now = lambda s: (0, jnp.minimum(s, HEADS - 1) // 4)
    before = lambda s: (0, jnp.maximum(s - 1, 0))
    return pl.pallas_call(
        behind(short_forward_kernel, len(deps), False),
        grid=(HEADS + 1,),
        in_specs=[ANYWHERE] * len(deps)
        + [
            pl.BlockSpec((count, GROUP), now),
            pl.BlockSpec((count, GROUP), now),
            whole((WIDTH, count)),
            whole((count, 1)),
            whole((1, count)),
        ],
        out_specs=[
            pl.BlockSpec((count, count), before),
            whole((WIDTH, count)),
            pl.BlockSpec((8, count), lambda s: (jnp.maximum(s - 1, 0), 0)),
            whole((count, WIDTH)),
        ],
        out_shape=[
            jax.ShapeDtypeStruct((count, HEADS * count), bf16),
            jax.ShapeDtypeStruct((WIDTH, count), f32),
            jax.ShapeDtypeStruct((HEADS * 8, count), f32),
            jax.ShapeDtypeStruct((count, WIDTH), bf16),
        ],
        scratch_shapes=[
            pltpu.VMEM((2, count, count), f32),
            pltpu.VMEM((count, count), f32),
            pltpu.VMEM((2, 8, count), f32),
        ],
        compiler_params=pltpu.CompilerParams(**PARAMS),
        cost_estimate=pl.CostEstimate(
            flops=12 * count * count * WIDTH, bytes_accessed=12 << 20, transcendentals=HEADS * count * count
        ),
        name="short_forward",
    )(*deps, q, k, vt, ids[:, None], ids[None, :])


CHIPS = 2


def long_prepare_kernel(
    depth, place_ref, own0, other0, own1, other1, w_ref, vec_ref, n1_ref, q_ref, k_ref, vt_ref,
    wk, wv,
):
    step = pl.program_id(0)
    core = place_ref[1]
    near = step < depth
    lanes = lambda base: pl.ds(pl.multiple_of(base + core * GROUP, GROUP), GROUP)

    @pl.when(step == 0)
    def _():
        for other in (0, 1):
            @pl.when(core == other)
            def _():
                wk[...] = w_ref[:, WIDTH + other * GROUP : WIDTH + (other + 1) * GROUP]
                wv[...] = w_ref[:, 2 * WIDTH + other * GROUP : 2 * WIDTH + (other + 1) * GROUP]

    chips = own0.shape[0]
    rows = jnp.concatenate(
        [jnp.where(near, a[chip], b[chip]) for chip in range(chips) for a, b in ((own0, own1), (other0, other1))],
        axis=0,
    )
    standard, _ = standardize(rows.astype(f32))
    normed = (standard * row_of(vec_ref, V_G1) + row_of(vec_ref, V_O1)).astype(bf16)
    n1_ref[...] = normed
    k = dot(normed, wk[...])
    v = dot(normed, wv[...]) + vec_ref[V_CONTENT : V_CONTENT + 1, lanes(0)]
    k_ref[...] = k.astype(bf16)
    vt_ref[...] = v.astype(bf16).T

    @pl.when(step == 0)
    def _():
        q = (dot(normed[:TILE, :], w_ref[:, lanes(0)]) + vec_ref[V_ASK : V_ASK + 1, lanes(0)]).astype(bf16)
        q_ref[...] = (q.astype(f32) * (1.0 / math.sqrt(HEAD))).astype(bf16)


def long_prepare(layout, place, stacks, weights, vectors, deps):
    depth = layout.depth
    total = 2 * depth * TILE
    steps = depth // CHIPS
    tile = CHIPS * TILE
    row_spec = pl.BlockSpec((tile, GROUP), lambda i, _: (i, 0))
    col_spec = pl.BlockSpec((GROUP, tile), lambda i, _: (0, i))
    near = pl.BlockSpec((CHIPS, LONG, WIDTH), lambda i, _: (jnp.minimum(i, steps - 1), 0, 0))
    far = pl.BlockSpec((CHIPS, LONG, WIDTH), lambda i, _: (jnp.maximum(i - steps, 0), 0, 0))
    flat = jax.ShapeDtypeStruct((total, GROUP), bf16)
    tall = jax.ShapeDtypeStruct((GROUP, total), bf16)
    return pl.pallas_call(
        behind(functools.partial(long_prepare_kernel, depth // CHIPS), len(deps)),
        grid_spec=pltpu.PrefetchScalarGridSpec(
            num_scalar_prefetch=1,
            grid=(2 * steps,),
            in_specs=[ANYWHERE] * len(deps)
            + [near, near, far, far, whole((WIDTH, 3 * WIDTH)), whole(vectors.shape)],
            out_specs=[
                pl.BlockSpec((tile, WIDTH), lambda i, _: (i, 0)),
                whole((TILE, GROUP)),
                row_spec,
                col_spec,
            ],
            scratch_shapes=[pltpu.VMEM((WIDTH, GROUP), bf16)] * 2,
        ),
        out_shape=[
            jax.ShapeDtypeStruct((total, WIDTH), bf16),
            jax.ShapeDtypeStruct((TILE, GROUP), bf16),
            flat,
            tall,
        ],
        compiler_params=pltpu.CompilerParams(**PARAMS),
        cost_estimate=pl.CostEstimate(
            flops=4 * total * WIDTH * GROUP, bytes_accessed=18 << 20, transcendentals=0
        ),
        name="long_prepare",
    )(place, *deps, *stacks, weights, vectors)


CHUNK = 256
BACK = 2 * TILE
PARTS = TILE // CHUNK
LOCAL_HEADS = GROUP // HEAD
STEPS = LOCAL_HEADS * PARTS


def long_forward_kernel(
    q_ref, k_ref, vt_ref, e_ref, o_ref, linv_ref, keep_ref, send_ref, s_ref, top_ref
):
    step = pl.program_id(0)
    total = k_ref.shape[0]
    tile = min(total, 4096)
    last = pl.num_programs(0) - 1

    def masked_queries():
        rows = pl.ds(pl.multiple_of(lax.rem(step, PARTS) * CHUNK, CHUNK), CHUNK)
        return head_lanes(q_ref[rows, :], step // PARTS)

    def first_tile(slot, low, masked, top):
        s = dot(k_ref[pl.ds(low, tile), :], masked, 1, 1)
        s_ref[slot, pl.ds(low, tile), :] = s
        return jnp.maximum(top, jnp.max(s.reshape(tile // 8, 8, CHUNK), axis=0))

    def second_tile(slot, low, top, head, carry):
        summed, mixed = carry
        e = jnp.exp(s_ref[slot, pl.ds(low, tile), :] - top)
        summed = summed + jnp.sum(e.reshape(tile // 8, 8, CHUNK), axis=0)
        low_e = e.astype(bf16)
        e_ref[pl.ds(low, tile), :] = low_e
        values = vt_ref[pl.ds(pl.multiple_of(head * HEAD, HEAD), HEAD), pl.ds(low, tile)]
        return summed, mixed + dot(values, low_e)

    start_top = jnp.full((8, CHUNK), -1e30, f32)
    start_sum = (jnp.zeros((8, CHUNK), f32), jnp.zeros((HEAD, CHUNK), f32))

    def finish(head, part, carry):
        summed, mixed = carry
        linv = 1.0 / column_sum(summed)
        linv_ref[...] = jnp.broadcast_to(linv, (8, CHUNK))
        o_ref[part, pl.ds(pl.multiple_of(head * HEAD, HEAD), HEAD), :] = mixed * linv

    def place(turn):
        return pl.multiple_of(turn * tile, tile)

    @pl.when(step == 0)
    def _():
        masked = masked_queries()
        top_ref[0] = lax.fori_loop(
            0, total // tile, lambda t, top: first_tile(0, place(t), masked, top), start_top
        )

    for parity in (0, 1):
        @pl.when((step > 0) & (step < last) & (lax.rem(step, 2) == parity))
        def _():
            masked = masked_queries()
            before = step - 1
            head = before // PARTS
            top_row = jnp.max(top_ref[1 - parity], axis=0, keepdims=True)

            def body(turn, carry):
                top, kept = carry
                low = place(turn)
                top = first_tile(parity, low, masked, top)
                kept = second_tile(1 - parity, low, top_row, head, kept)
                return top, kept

            top, kept = lax.fori_loop(0, total // tile, body, (start_top, start_sum))
            top_ref[parity] = top
            finish(head, lax.rem(before, PARTS), kept)

    @pl.when(step == last)
    def _():
        slot = (STEPS - 1) % 2
        top_row = jnp.max(top_ref[slot], axis=0, keepdims=True)
        head = LOCAL_HEADS - 1
        kept = lax.fori_loop(
            0,
            total // tile,
            lambda t, carry: second_tile(slot, place(t), top_row, head, carry),
            start_sum,
        )
        finish(head, PARTS - 1, kept)
        keep_ref[...] = o_ref[0].T.astype(bf16)
        send_ref[...] = o_ref[1].T.astype(bf16)


def long_forward(q, k, vt):
    total = k.shape[0]
    before = lambda s: jnp.maximum(s - 1, 0)
    half = jax.ShapeDtypeStruct((CHUNK, GROUP), bf16)
    return pl.pallas_call(
        long_forward_kernel,
        grid=(STEPS + 1,),
        in_specs=[once((TILE, GROUP)), once((total, GROUP)), once((GROUP, total))],
        out_specs=[
            pl.BlockSpec((total, CHUNK), lambda s: (0, before(s))),
            whole((PARTS, GROUP, CHUNK)),
            pl.BlockSpec((8, CHUNK), lambda s: (before(s), 0)),
            whole((CHUNK, GROUP)),
            whole((CHUNK, GROUP)),
        ],
        scratch_shapes=[pltpu.VMEM((2, total, CHUNK), f32), pltpu.VMEM((2, 8, CHUNK), f32)],
        out_shape=[
            jax.ShapeDtypeStruct((total, STEPS * CHUNK), bf16),
            jax.ShapeDtypeStruct((PARTS, GROUP, CHUNK), f32),
            jax.ShapeDtypeStruct((STEPS * 8, CHUNK), f32),
            half,
            half,
        ],
        compiler_params=pltpu.CompilerParams(**PARAMS),
        cost_estimate=pl.CostEstimate(
            flops=16 * TILE * total * GROUP, bytes_accessed=24 << 20, transcendentals=4 * TILE * total
        ),
        name="long_forward",
    )(q, k, vt)


def feed_kernel(layout, place_ref, x_ref, ids_ref, g_ref, mine_ref, other_ref, short_ref, vec_ref, hid_ref, *refs):
    count = len(layout.gathered_specs(SECOND))
    pieces, refs = refs[:count], refs[count:]
    out_ref, midl_ref, mids_ref, keep_ref, send_ref, das_ref, row_ref, hsum_ref = refs[:8]
    grads = refs[8:-8]
    wp_ref, we_ref, wr_ref, gp_ref, ge_ref, gr_ref, act_ref, dh_ref = refs[-8:]
    swapped = place_ref[1] == 1

    def visit(block, rows):
        span = pl.ds(pl.multiple_of(block * 16, 16), 16)
        wp_ref[span, :] = rows[:, :WIDTH]
        we_ref[span, :] = rows[:, WIDTH : WIDTH + FF]
        for k in range(4):
            low = WIDTH + FF + k * WIDTH
            wr_ref[pl.ds(pl.multiple_of(block * 64 + 16 * k, 16), 16), :] = rows[:, low : low + WIDTH]

    layout.each_gathered(place_ref, pieces, visit)

    x = x_ref[...].astype(f32)
    live = (ids_ref[...] >= 0).astype(f32)
    upstream = g_ref[...].astype(f32)
    mine, other = mine_ref[...], other_ref[...]
    long = jnp.concatenate([jnp.where(swapped, other, mine), jnp.where(swapped, mine, other)], axis=1)
    attended = jnp.concatenate([long, short_ref[...]], axis=0)
    branch = dot(attended, wp_ref[...]) + row_of(vec_ref, V_MIXER)
    middle = x + live * branch
    standard, inverse = standardize(middle)
    gain = row_of(vec_ref, V_G2)
    normed = (standard * gain + row_of(vec_ref, V_O2)).astype(bf16)
    branch_low = (live * upstream).astype(bf16)

    part = 256

    def products(low):
        return (
            dot(normed, we_ref[:, low : low + part]) + hid_ref[:, low : low + part],
            dot(branch_low, wr_ref[low : low + part, :], 1, 1),
        )

    following = products(0)
    for low in range(0, FF, part):
        hidden, into = following
        if low + part < FF:
            following = products(low + part)
        square = hidden * hidden
        tangent = jnp.tanh(hidden * (gelu_scale + (gelu_scale * 0.044715) * square))
        half = 0.5 + 0.5 * tangent
        active = (hidden * half).astype(bf16)
        slope = half + (0.5 * hidden) * (1.0 - tangent * tangent) * (
            gelu_scale + (gelu_scale * 3.0 * 0.044715) * square
        )
        hidden_low = (into * slope).astype(bf16)
        hsum_ref[:, low : low + part] = column_sum(hidden_low.astype(f32))
        act_ref[:, low : low + part] = active
        dh_ref[:, low : low + part] = hidden_low
        gr_ref[low : low + part, :] = dot(active, branch_low, 0, 0).astype(bf16)
        ge_ref[:, low : low + part] = dot(normed, hidden_low, 0, 0).astype(bf16)

    branch_two = dot(act_ref[...], wr_ref[...]) + row_of(vec_ref, V_NARROW)
    out_ref[...] = (middle + live * branch_two).astype(bf16)
    normed_grad = dot(dh_ref[...], we_ref[...], 1, 1)
    middle_grad = upstream + norm_backward(normed_grad, standard, inverse, gain)
    midl_ref[...] = middle_grad[:LONG, :]
    mids_ref[...] = middle_grad[LONG:, :]
    attn_low = (live * middle_grad).astype(bf16)
    attended_grad = dot(attn_low, wp_ref[...], 1, 1).astype(bf16)
    das_ref[...] = attended_grad[LONG:, :]
    left, right = attended_grad[:LONG, :GROUP], attended_grad[:LONG, GROUP:]
    keep_ref[...] = jnp.where(swapped, right, left)
    send_ref[...] = jnp.where(swapped, left, right)
    gp_ref[...] = dot(attended, attn_low, 0, 0).astype(bf16)
    row_ref[...] = jnp.zeros_like(row_ref)
    row_ref[0:1, :] = column_sum(attn_low.astype(f32))
    row_ref[1:2, :] = column_sum(branch_low.astype(f32))
    row_ref[2:3, :] = column_sum(normed_grad * standard)
    row_ref[3:4, :] = column_sum(normed_grad)

    def take(block):
        span = pl.ds(pl.multiple_of(block * 16, 16), 16)
        parts = [gp_ref[span, :], ge_ref[span, :]] + [
            gr_ref[pl.ds(pl.multiple_of(block * 64 + 16 * k, 16), 16), :] for k in range(4)
        ]
        return jnp.concatenate(parts, axis=1)

    layout.store_scattered(place_ref, grads, take)


def feed(layout, place, rows, ids, upstream, mine, other, short, vectors, hidden_shift, pieces):
    count = rows.shape[0]
    grads = layout.scattered_shapes(SECOND)
    operands = [rows, ids[:, None], upstream, mine, other, short, vectors, hidden_shift]
    shapes = [
        jax.ShapeDtypeStruct((count, WIDTH), bf16),
        jax.ShapeDtypeStruct((LONG, WIDTH), f32),
        jax.ShapeDtypeStruct((count - LONG, WIDTH), f32),
        jax.ShapeDtypeStruct((LONG, GROUP), bf16),
        jax.ShapeDtypeStruct((LONG, GROUP), bf16),
        jax.ShapeDtypeStruct((count - LONG, WIDTH), bf16),
        jax.ShapeDtypeStruct((8, WIDTH), f32),
        jax.ShapeDtypeStruct((1, FF), f32),
    ] + grads
    return pl.pallas_call(
        functools.partial(feed_kernel, layout),
        grid_spec=pltpu.PrefetchScalarGridSpec(
            num_scalar_prefetch=1,
            grid=(1,),
            in_specs=[once(x.shape) for x in operands] + layout.gathered_specs(SECOND),
            out_specs=[once(x.shape) for x in shapes],
            scratch_shapes=[
                pltpu.VMEM((WIDTH, WIDTH), bf16),
                pltpu.VMEM((WIDTH, FF), bf16),
                pltpu.VMEM((FF, WIDTH), bf16),
                pltpu.VMEM((WIDTH, WIDTH), bf16),
                pltpu.VMEM((WIDTH, FF), bf16),
                pltpu.VMEM((FF, WIDTH), bf16),
                pltpu.VMEM((count, FF), bf16),
                pltpu.VMEM((count, FF), bf16),
            ],
        ),
        out_shape=shapes,
        compiler_params=pltpu.CompilerParams(**PARAMS),
        cost_estimate=pl.CostEstimate(
            flops=6 * count * WIDTH * (WIDTH + 2 * FF), bytes_accessed=18 << 20, transcendentals=count * FF
        ),
        name="feed",
    )(place, *operands, *pieces)


def long_backward_kernel(
    final, place_ref, e_ref, k_ref, vt_ref, n1_ref, q_ref, mine_ref, other_ref, o_ref, linv_ref, w_ref, vec_ref,
    *refs,
):
    if final:
        dq_in, gkv_in, row_in, side_in, *refs = refs
    (
    keep_ref, send_ref, gq_ref, dq_acc, gkv_ref, row_ref, side_ref,
    qblk, dblk, delta, ds_ref, wq, wkv,
    ) = refs
    step = pl.program_id(0)
    core = place_ref[1]

    @pl.when(step == 0)
    def _():
        lanes = lambda base: pl.ds(pl.multiple_of(base + core * GROUP, GROUP), GROUP)
        wq[...] = w_ref[:, lanes(0)]
        wkv[:, :GROUP] = w_ref[:, lanes(WIDTH)]
        wkv[:, GROUP:] = w_ref[:, lanes(2 * WIDTH)]
        if final:
            dq_acc[...] = dq_in[...]
            gkv_ref[...] = gkv_in[...]
            row_ref[...] = row_in[...]
            side_ref[...] = side_in[...]
        else:
            for ref in (dq_acc, gkv_ref, row_ref, side_ref):
                ref[...] = jnp.zeros_like(ref)
        for part in range(PARTS):
            rows = slice(part * CHUNK, (part + 1) * CHUNK)
            turned = (mine_ref, other_ref)[part][...].astype(f32).T
            product = turned * o_ref[part]
            pieces = []
            for head in range(LOCAL_HEADS):
                index = head * PARTS + part
                span = slice(head * HEAD, (head + 1) * HEAD)
                linv = linv_ref[8 * index : 8 * index + 1, :]
                delta[8 * index : 8 * index + 8, :] = jnp.broadcast_to(
                    column_sum(product[span, :]) * linv, (8, CHUNK)
                )
                pieces.append(turned[span, :] * linv)
            scaled = jnp.concatenate(pieces, axis=0).T
            for head in range(LOCAL_HEADS):
                index = head * PARTS + part
                span = slice(index * CHUNK, (index + 1) * CHUNK)
                dblk[span, :] = head_lanes(scaled, head)
                qblk[span, :] = head_lanes(q_ref[rows, :], head)

    def span_of(index):
        return slice(index * CHUNK, (index + 1) * CHUNK)

    v = vt_ref[...].T
    kt = k_ref[...].T
    slopes = dot(v, dblk[span_of(0), :], 1, 1)
    for index in range(STEPS):
        head, part = index // PARTS, index % PARTS
        span = span_of(index)
        following = dot(v, dblk[span_of(index + 1), :], 1, 1) if index + 1 < STEPS else None
        ds = (
            e_ref[:, span].astype(f32) * (slopes - delta[8 * index : 8 * index + 1, :])
        ).astype(bf16)
        ds_ref[:, span] = ds
        own = slice(head * HEAD, (head + 1) * HEAD)
        dq_acc[part, own, :] += dot(kt[own, :], ds)
        slopes = following

    value_grad = dot(e_ref[...], dblk[...]).astype(bf16)
    key_grad = dot(ds_ref[...], qblk[...]).astype(bf16)
    both = jnp.concatenate([key_grad, value_grad], axis=1)
    normed = n1_ref[...]
    through = dot(both, wkv[...], 1, 1)
    gkv_ref[...] += dot(normed, both, 0, 0)
    side_ref[1:2, :] += column_sum(value_grad.astype(f32))

    def put(entire):
        low = entire.astype(bf16)
        for chip in range(BACK // TILE):
            base = chip * TILE
            keep_ref[chip] = low[base : base + LONG, :]
            send_ref[chip] = low[base + LONG : base + TILE, :]
        shifts = column_sum(entire)
        scales = column_sum(entire * normed.astype(f32)) - shifts * row_of(vec_ref, V_O1)
        row_ref[0:1, :] += scales / row_of(vec_ref, V_G1)
        row_ref[1:2, :] += shifts

    if not final:
        put(through)
        return
    last = pl.num_programs(0) - 1

    @pl.when(step < last)
    def _():
        put(through)

    @pl.when(step == last)
    def _():
        query_grad = jnp.concatenate(
            [dq_acc[part].T for part in range(PARTS)], axis=0
        ) * (1.0 / math.sqrt(HEAD))
        low = query_grad.astype(bf16)
        put(jnp.concatenate([through[:TILE, :] + dot(low, wq[...], 1, 1), through[TILE:, :]], axis=0))
        gq_ref[...] = dot(normed[:TILE, :], low, 0, 0)
        side_ref[0:1, :] += column_sum(low.astype(f32))


def long_backward(layout, final, place, e, k, vt, normed, q, mine, other, o, linv, weights, vectors, sums, deps):
    tiles = layout.depth * TILE // BACK
    away = (lambda i: i) if not final else (lambda i: lax.rem(i + 1, tiles))
    turn = lambda i: away(i) if final else tiles + i
    out = jax.ShapeDtypeStruct((layout.depth, LONG, WIDTH), bf16)
    out_spec = pl.BlockSpec((BACK // TILE, LONG, WIDTH), lambda i, p: (away(i), 0, 0))
    sum_shapes = [
        jax.ShapeDtypeStruct((PARTS, GROUP, CHUNK), f32),
        jax.ShapeDtypeStruct((WIDTH, 2 * GROUP), f32),
        jax.ShapeDtypeStruct((8, WIDTH), f32),
        jax.ShapeDtypeStruct((8, GROUP), f32),
    ]
    sum_specs = [whole(x.shape) for x in sum_shapes]
    return pl.pallas_call(
        behind(functools.partial(long_backward_kernel, final), len(deps)),
        grid_spec=pltpu.PrefetchScalarGridSpec(
            num_scalar_prefetch=1,
            grid=(tiles,),
            in_specs=[ANYWHERE] * len(deps)
            + [
                pl.BlockSpec((BACK, STEPS * CHUNK), lambda i, p: (turn(i), 0)),
                pl.BlockSpec((BACK, GROUP), lambda i, p: (turn(i), 0)),
                pl.BlockSpec((GROUP, BACK), lambda i, p: (0, turn(i))),
                pl.BlockSpec((BACK, WIDTH), lambda i, p: (turn(i), 0)),
                whole((TILE, GROUP)),
                whole((CHUNK, GROUP)),
                whole((CHUNK, GROUP)),
                whole((PARTS, GROUP, CHUNK)),
                whole((STEPS * 8, CHUNK)),
                once((WIDTH, 3 * WIDTH)),
                whole(vectors.shape),
            ]
            + sum_specs[: len(sums)],
            out_specs=[out_spec, out_spec, whole((WIDTH, GROUP))] + sum_specs,
            scratch_shapes=[
                pltpu.VMEM((STEPS * CHUNK, GROUP), bf16),
                pltpu.VMEM((STEPS * CHUNK, GROUP), bf16),
                pltpu.VMEM((STEPS * 8, CHUNK), f32),
                pltpu.VMEM((BACK, STEPS * CHUNK), bf16),
                pltpu.VMEM((WIDTH, GROUP), bf16),
                pltpu.VMEM((WIDTH, 2 * GROUP), bf16),
            ],
        ),
        out_shape=[out, out, jax.ShapeDtypeStruct((WIDTH, GROUP), f32)] + sum_shapes,
        compiler_params=pltpu.CompilerParams(**PARAMS),
        cost_estimate=pl.CostEstimate(
            flops=20 * TILE * k.shape[0] * GROUP, bytes_accessed=16 << 20, transcendentals=0
        ),
        name="long_backward_final" if final else "long_backward",
    )(place, *deps, e, k, vt, normed, q, mine, other, o, linv, weights, vectors, *sums)


def short_backward_kernel(
    layout, place_ref, e_ref, k_ref, v_ref, q_ref, kt_ref, da_ref, o_ref, linv_ref, n1_ref, x_ref, mid_ref, w_ref,
    vec_ref, gq_ref, gkv_ref, lrow_ref, lside_ref, frow_ref, hsum_ref,
    dx_ref, *refs,
):
    grads = refs[:-9]
    scaled, delta, dblk, qblk, ds_ref, dqt, dqkv, packed, column = refs[-9:]
    step = pl.program_id(0)
    count = k_ref.shape[0]

    @pl.when(step == 0)
    def _():
        for low in range(0, WIDTH, GROUP):
            turned = da_ref[:, low : low + GROUP].astype(f32).T
            product = turned * o_ref[low : low + GROUP, :]
            pieces = []
            for head in range(4):
                span = slice(head * HEAD, (head + 1) * HEAD)
                index = low // HEAD + head
                linv = linv_ref[8 * index : 8 * index + 1, :]
                delta[8 * index : 8 * index + 8, :] = jnp.broadcast_to(
                    column_sum(product[span, :]) * linv, (8, count)
                )
                pieces.append(turned[span, :] * linv)
            scaled[:, low : low + GROUP] = jnp.concatenate(pieces, axis=0).T.astype(bf16)

    def group(side):
        low = side * GROUP
        for head in range(4):
            index = side * 4 + head
            span = slice(head * count, (head + 1) * count)
            own = slice(head * HEAD, (head + 1) * HEAD)
            dblk[span, :] = head_lanes(scaled[:, low : low + GROUP], head)
            qblk[span, :] = head_lanes(q_ref[...], head)
            slopes = dot(v_ref[...], dblk[span, :], 1, 1)
            ds = (
                e_ref[:, span].astype(f32) * (slopes - delta[8 * index : 8 * index + 1, :])
            ).astype(bf16)
            ds_ref[:, span] = ds
            dqt[own, :] = dot(kt_ref[low + head * HEAD : low + (head + 1) * HEAD, :], ds)
        value_grad = dot(e_ref[...], dblk[...])
        key_grad = dot(ds_ref[...], qblk[...])
        query_grad = dqt[...].T * (1.0 / math.sqrt(HEAD))
        dqkv[:, low : low + GROUP] = query_grad.astype(bf16)
        dqkv[:, WIDTH + low : WIDTH + low + GROUP] = key_grad.astype(bf16)
        dqkv[:, 2 * WIDTH + low : 2 * WIDTH + low + GROUP] = value_grad.astype(bf16)

    for side in (0, 1):
        pl.when(step == side)(functools.partial(group, side))

    @pl.when(step == 1)
    def _():
        rows_grad = dot(dqkv[...], w_ref[...], 1, 1)
        standard, inverse = standardize(x_ref[LONG:, :].astype(f32))
        through = norm_backward(rows_grad, standard, inverse, row_of(vec_ref, V_G1))
        dx_ref[...] = (mid_ref[...] + through).astype(bf16)
        core = place_ref[1]
        column[...] = jnp.zeros_like(column)
        column[0:1, :] = column_sum(dqkv[:, :WIDTH].astype(f32))
        column[1:2, :] = column_sum(dqkv[:, 2 * WIDTH :].astype(f32))
        for other in (0, 1):
            @pl.when(core == other)
            def _():
                span = slice(other * GROUP, (other + 1) * GROUP)
                column[0:2, span] += lside_ref[0:2, :]
        column[2:4, :] = frow_ref[0:2, :]
        column[4:5, :] = lrow_ref[0:1, :] + column_sum(rows_grad * standard)
        column[5:6, :] = lrow_ref[1:2, :] + column_sum(rows_grad)
        column[6:8, :] = frow_ref[2:4, :]
        packed[:, 3 * WIDTH :] = column[...].T
        if layout.pieces:
            shard = 4 * layout.rows
            for index in range(layout.shards):
                low = index * layout.rows
                packed[low : low + 1, FIRST - shard :] = hsum_ref[:, index * shard : (index + 1) * shard]
        packed[:, : 3 * WIDTH] = dot(n1_ref[...], dqkv[...], 0, 0)
        for other in (0, 1):
            @pl.when(core == other)
            def _():
                for third in range(3):
                    low = third * WIDTH + other * GROUP
                    extra = gq_ref[...] if third == 0 else gkv_ref[:, (third - 1) * GROUP : third * GROUP]
                    packed[:, low : low + GROUP] += extra

        layout.store_scattered(
            place_ref, grads, lambda block: packed[pl.ds(pl.multiple_of(block * 16, 16), 16), :].astype(bf16)
        )


def short_backward(
    layout, place, e, k, v, q, kt, da, o, linv, n1, rows, mid, weights, vectors, gq, gkv, lrow, lside, frow, hsum, deps
):
    count = k.shape[0]
    half = pl.BlockSpec((count, GROUP), lambda i, _: (0, i))
    grads = layout.scattered_shapes(FIRST)
    return pl.pallas_call(
        behind(functools.partial(short_backward_kernel, layout), len(deps)),
        grid_spec=pltpu.PrefetchScalarGridSpec(
            num_scalar_prefetch=1,
            grid=(2,),
            in_specs=[ANYWHERE] * len(deps)
            + [
                pl.BlockSpec((count, 4 * count), lambda i, _: (0, i)),
                half,
                half,
                half,
                once((WIDTH, count)),
                once((count, WIDTH)),
                once((WIDTH, count)),
                once((HEADS * 8, count)),
                once((count, WIDTH)),
                once(rows.shape),
                once((count, WIDTH)),
                once((WIDTH, 3 * WIDTH)),
                whole(vectors.shape),
                once((WIDTH, GROUP)),
                once((WIDTH, 2 * GROUP)),
                whole((8, WIDTH)),
                whole((8, GROUP)),
                whole((8, WIDTH)),
                whole((1, FF)),
            ],
            out_specs=[once((count, WIDTH))] + [once(g.shape) for g in grads],
            scratch_shapes=[
                pltpu.VMEM((count, WIDTH), bf16),
                pltpu.VMEM((HEADS * 8, count), f32),
                pltpu.VMEM((4 * count, GROUP), bf16),
                pltpu.VMEM((4 * count, GROUP), bf16),
                pltpu.VMEM((count, 4 * count), bf16),
                pltpu.VMEM((GROUP, count), f32),
                pltpu.VMEM((count, 3 * WIDTH), bf16),
                pltpu.VMEM((WIDTH, FIRST), f32),
                pltpu.VMEM((SIDE, WIDTH), f32),
            ],
        ),
        out_shape=[jax.ShapeDtypeStruct((count, WIDTH), bf16)] + grads,
        compiler_params=pltpu.CompilerParams(**PARAMS),
        cost_estimate=pl.CostEstimate(
            flops=24 * count * count * WIDTH, bytes_accessed=18 << 20, transcendentals=0
        ),
        name="short_backward",
    )(place, *deps, e, k, v, q, kt, da, o, linv, n1, rows, mid, weights, vectors, gq, gkv, lrow, lside, frow, hsum)


def per_device(
    incoming_rows,
    picture_label,
    triple_kernel,
    mixer_kernel,
    widening_kernel,
    narrowing_kernel,
    asker_offset,
    content_offset,
    mixer_offset_vector,
    widening_offset,
    narrowing_offset,
    leading_gain,
    leading_offset,
    second_gain,
    second_offset,
    loss_sensitivity,
):
    layout = Layout(lax.axis_size("band"), lax.axis_size("batch"))
    band = lax.axis_index("band")
    rows = incoming_rows[0]
    ids = picture_label[0]
    upstream = loss_sensitivity[0]
    shard = layout.rows
    place = jnp.stack([band // 2, band % 2, band // 4, (band // 2) % 2, lax.axis_index("batch")]).astype(jnp.int32)

    small = (
        asker_offset,
        content_offset,
        mixer_offset_vector,
        narrowing_offset,
        leading_gain,
        leading_offset,
        second_gain,
        second_offset,
    )
    if layout.pieces:
        first_stack = layout.gather_depth(pack_first(triple_kernel, small, widening_offset))
        first_plane = layout.gather_plane(first_stack)
        near = layout.gather_depth(pack_rows(rows, (first_stack,)), tuple(first_plane[1:]))
        first = layout.gather_core(first_plane)
    else:
        near = layout.gather_depth(rows[:LONG])
        columns = [v.astype(bf16)[:, None] for v in small]
        columns += [jnp.zeros((shard, SIDE - 12), bf16), widening_offset.astype(bf16).reshape(shard, 4)]
        first = layout.gather_whole(jnp.concatenate([triple_kernel.astype(bf16)] + columns, axis=1))
        second_stack = layout.gather_whole(
            jnp.concatenate([mixer_kernel.astype(bf16), widening_kernel.astype(bf16)], axis=1)
        )[0]
        narrow = layout.gather_whole(narrowing_kernel.astype(bf16))[0]
        narrow = narrow.reshape(WIDTH // 16, 4, 16, WIDTH).transpose(0, 2, 1, 3).reshape(WIDTH, FF)
        second = [jnp.concatenate([second_stack, narrow], axis=1)]
    far = layout.flip(near, 2)

    n1, q_s, k_s, v_s, kt_s, vt_s, wqkv, vectors, hidden_shift = short_qkv(layout, place, rows, first)
    if layout.pieces:
        packed = pack_second(mixer_kernel, widening_kernel, narrowing_kernel, (n1,))
    else:
        hidden_shift = first[0][:, FIRST - 4 :].reshape(1, FF).astype(f32)
        packed = second[0]
    e_s, o_s, linv_s, att_s = short_forward(q_s, k_s, vt_s, ids[LONG:], (near, packed))
    if layout.pieces:
        second_stack = layout.gather_depth(packed, (linv_s,))
        second_plane = layout.gather_plane(second_stack)
    (far,) = tie([far], (second_stack,))
    stacks = (near, layout.flip(near, 1), far, layout.flip(far, 1))
    n1_l, q_l, k_l, vt_l = long_prepare(layout, place, stacks, wqkv, vectors, (second_stack,))

    e_l, o_l, linv_l, att_keep, att_send = long_forward(q_l, k_l, vt_l)
    if layout.pieces:
        second = layout.gather_core(second_plane[:1] + list(tie(second_plane[1:], (att_keep,))))
    layer_out, mid_l, mid_s, da_keep, da_send, da_s, feed_rows, hidden_sum, *second_grads = feed(
        layout, place, rows, ids, upstream, att_keep, layout.flip(att_send, 1), att_s, vectors, hidden_shift, second
    )
    da_other = layout.flip(da_send, 1)
    inputs = (place, e_l, k_l, vt_l, n1_l, q_l, da_keep, da_other, o_l, linv_l, wqkv, vectors)

    pairs = layout.scatter_core(second_grads) if layout.pieces else []
    keep_x, send_x, _, *sums = long_backward(layout, False, *inputs, (), tuple(pairs[1:]))
    moved = (keep_x.astype(f32) + layout.flip(send_x, 1).astype(f32)).astype(bf16)
    totals = layout.scatter_plane(pairs) if layout.pieces else []
    keep, send, gq, _, gkv, long_sums, long_side = long_backward(
        layout, True, *inputs, sums, (moved, *totals[1:])
    )
    dx_totals = layout.add_depth([keep, layout.flip(send, 1), layout.flip(moved, 2)])
    dx_s, *first_grads = short_backward(
        layout, place, e_s, k_s, v_s, q_s, kt_s, da_s, o_s, linv_s, n1, rows, mid_s, wqkv, vectors,
        gq, gkv, long_sums, long_side, feed_rows, hidden_sum, tuple(dx_totals[1:]),
    )
    dx_long = layout.scatter_depth(dx_totals, -1)
    if layout.pieces:
        second_grad = layout.scatter_depth(totals)
        narrow_grad = second_grad[:, WIDTH + FF :].reshape(shard, 4, WIDTH).transpose(1, 0, 2)
        narrow_grad = narrow_grad.reshape(4 * shard, WIDTH)
        first_grad = layout.scatter_depth(layout.scatter_plane(layout.scatter_core(first_grads)))
        hidden_grad = first_grad[0, FIRST - 4 * shard :]
    else:
        packed = second_grads[0][:, WIDTH + FF :].reshape(WIDTH // 16, 16, 4, WIDTH).transpose(0, 2, 1, 3)
        narrow_grad = layout.scatter_whole(packed.reshape(FF, WIDTH))
        second_grad = layout.scatter_whole(second_grads[0][:, : WIDTH + FF])
        first_grad = layout.scatter_whole(first_grads[0])
        hidden_grad = layout.scatter_whole(hidden_sum[0])
    small = first_grad[:, 3 * WIDTH :]

    standard, inverse = standardize(rows[:LONG].astype(f32))
    dx_l = (mid_l + norm_backward(dx_long, standard, inverse, vectors[V_G1][None, :])).astype(bf16)
    input_grad = jnp.concatenate([dx_l, dx_s], axis=0)
    return (
        layer_out[None],
        input_grad[None],
        first_grad[:, : 3 * WIDTH],
        second_grad[:, :WIDTH],
        second_grad[:, WIDTH : WIDTH + FF],
        narrow_grad,
        small[:, 0],
        small[:, 1],
        small[:, 2],
        hidden_grad,
        small[:, 3],
        small[:, 4],
        small[:, 5],
        small[:, 6],
        small[:, 7],
    )


def solution(mesh):
    shards = P(("band", "batch"))
    tokens = P("batch", "band", None)
    kernels = P(("band", "batch"), None)
    in_specs = (
        (tokens, P("batch", "band")) + (kernels,) * 4 + (shards,) * 9 + (tokens,)
    )
    out_specs = (tokens, tokens) + (kernels,) * 4 + (shards,) * 9
    return jax.shard_map(
        per_device, mesh=mesh, in_specs=in_specs, out_specs=out_specs, check_vma=False
    )
```

profile of v0, /device:TPU:0, one launch (start us, length us, event | category | flops | bytes accessed | tf_op | source)
XLA Modules:
  0.0 264.0 jit_solution(17826640366919558122)
XLA Ops:
  0.7 1.7 pack_first.1.refs_0_
  2.3 3.0 %collective-permute-start = (bf16[16,1664]{1,0:T(8,128)(2,1)}, bf16[16,1664]{1,0:T(8,128)(2,1)S(1)}, u32[]{:S(2)}, u32[]{:S(2)}) collective-permute-start(bf16[16,1664]{1,0:T(8,128)(2,1)} %pack_first.1.refs_0_), channel_id=1, source_target_pairs={{0,8},{2,10},{4,12},{6,14},{8,16},{10,18},{12,20},{14,22},{16,24},... | collective-permute-start | bytes 159752 | tf_op jit(solution)/shard_map/ppermute | solution.py:102
  5.3 2.6 collective-permute-start.1
  7.9 1.3 collective-permute-start.2
  9.8 2.1 collective-permute-done.1.refs_2_
  13.2 1.6 stack_blocks.3.refs_0_
  14.8 1.9 collective-permute-start.3
  16.7 1.7 pack_rows.1.refs_3_
  18.8 2.6 collective-permute-start.7
  21.4 1.0 collective-permute-start.8
  22.5 1.5 collective-permute-start.4
  24.4 4.9 %collective-permute-done.4.refs_1_.refs_2_ = bf16[4,16,1664]{2,1,0:T(8,128)(2,1)S(1)} collective-permute-done((bf16[4,16,1664]{2,1,0:T(8,128)(2,1)}, bf16[4,16,1664]{2,1,0:T(8,128)(2,1)S(1)}, u32[]{:S(2)}, u32[]{:S(2)}) %collective-permute-start.4) | collective-permute-done | bytes 213024 | tf_op jit(solution)/shard_map/ppermute | solution.py:112
  29.2 2.8 %collective-permute-done.5.refs_2_.refs_3_ = bf16[4,16,1664]{2,1,0:T(8,128)(2,1)S(1)} collective-permute-done((bf16[4,16,1664]{2,1,0:T(8,128)(2,1)}, bf16[4,16,1664]{2,1,0:T(8,128)(2,1)S(1)}, u32[]{:S(2)}, u32[]{:S(2)}) %collective-permute-start.5) | collective-permute-done | bytes 213024 | tf_op jit(solution)/shard_map/ppermute | solution.py:112
  32.1 5.7 %collective-permute-done.7.refs_5_ = bf16[256,512]{1,0:T(8,128)(2,1)S(1)} collective-permute-done((bf16[256,512]{1,0:T(8,128)(2,1)}, bf16[256,512]{1,0:T(8,128)(2,1)S(1)}, u32[]{:S(2)}, u32[]{:S(2)}) %collective-permute-start.7) | collective-permute-done | bytes 262176 | tf_op jit(solution)/shard_map/ppermute | solution.py:102
  39.1 2.2 stack_blocks.4.refs_0_.refs_2_
  41.4 1.5 collective-permute-start.17
  44.5 0.9 copy.36.refs_5_
  47.6 6.9 %short_qkv.1 = (bf16[768,512]{1,0:T(8,128)(2,1)}, bf16[768,512]{1,0:T(8,128)(2,1)}, bf16[768,512]{1,0:T(8,128)(2,1)}, bf16[768,512]{1,0:T(8,128)(2,1)}, bf16[512...) custom-call(s32[5]{0:T(128)} %stack.23.place_ref.refs_0_, ...), custom_call_target="tpu_custom_call" | custom-call | flops 1207959552 | bytes 10485760 | tf_op jit(solution)/shard_map/short_qkv/pallas_call | solution.py:315
  54.4 1.7 pack_second.1.refs_1_
  56.1 5.4 %collective-permute-start.13 = (bf16[16,4608]{1,0:T(8,128)(2,1)}, bf16[16,4608]{1,0:T(8,128)(2,1)S(1)}, u32[]{:S(2)}, u32[]{:S(2)}) collective-permute-start(bf16[16,4608]{1,0:T(8,128)(2,1)} %pack_second.1.refs_1_), channel_id=1, source_target_pairs={{0,8},{2,10},{4,12},{6,14},{8,16},{10,18},{12,20},{14,22},{16,24},... | collective-permute-start | bytes 442376 | tf_op jit(solution)/shard_map/ppermute | solution.py:102
  61.5 1.1 collective-permute-start.14
  62.6 1.7 collective-permute-start.15
  64.3 12.4 %short_forward.1 = (bf16[768,6144]{1,0:T(8,128)(2,1)}, f32[512,768]{1,0:T(8,128)}, f32[64,768]{1,0:T(8,128)}, bf16[768,512]{1,0:T(8,128)(2,1)}) custom-call(bf16[4,256,512]{2,1,0:T(8,128)(2,1)} %stack_blocks.4.refs_0_.refs_2_, bf16[16,4608]{1,0:T(8,128)(2,1)} %pack_second.1.refs_1_, bf16[768,512]{1,0:T(8,128)(2,1)} %get-tuple-element.66.refs_2_.refs_7_, ...), custom_call_target="tpu_custom_call" | custom-call | flops 3623878656 | bytes 12582912 | tf_op jit(solution)/shard_map/short_forward/pallas_call | solution.py:400
  77.5 2.0 stack_blocks.5.refs_1_.refs_0_
  79.5 1.0 copy-done.5
  81.5 1.1 collective-permute-start.21
  82.6 1.9 collective-permute-start.22
  84.5 1.0 copy-done.33
  85.4 10.6 %long_prepare.1 = (bf16[4096,512]{1,0:T(8,128)(2,1)}, bf16[512,256]{1,0:T(8,128)(2,1)}, bf16[4096,256]{1,0:T(8,128)(2,1)}, bf16[256,4096]{1,0:T(8,128)(2,1)}) custom-call(s32[5]{0:T(128)} %stack.23.place_ref.refs_0_, bf16[4,16,4608]{2,1,0:T(8,128)(2,1)} %stack_blocks.5.refs_1_.refs_0_, bf16[4,256,512]{2,1,0:T(8,128)(2,1)} %stack_blocks.4.refs_0_.refs_2_, ...), custom_call_target="tpu_custom_call" | custom-call | flops 2147483648 | bytes 18874368 | tf_op jit(solution)/shard_map/long_prepare/pallas_call | solution.py:486
  96.0 15.0 %long_forward.1 = (bf16[4096,2048]{1,0:T(8,128)(2,1)}, f32[2,256,256]{2,1,0:T(8,128)}, f32[64,256]{1,0:T(8,128)}, bf16[256,256]{1,0:T(8,128)(2,1)}, bf16[256,256]{1,0:T(8,128)(2,1)}) custom-call(bf16[512,256]{1,0:T(8,128)(2,1)} %get-tuple-element.72.q_ref.refs_8_.refs_9_, bf16[4096,256]{1,0:T(8,128)(2,1)} %get-tuple-element.73.k_ref.refs_5_.refs_6_, ...), custom_call_target="tpu_custom_call" | custom-call | flops 8589934592 | bytes 25165824 | tf_op jit(solution)/shard_map/long_forward/pallas_call | solution.py:606
  113.3 1.0 copy.37.ids_ref
  114.3 2.2 collective-permute-done.19.other_ref
  117.8 25.2 %feed.1 = (bf16[1024,512]{1,0:T(8,128)(2,1)}, f32[256,512]{1,0:T(8,128)}, f32[768,512]{1,0:T(8,128)}, bf16[256,256]{1,0:T(8,128)(2,1)}, bf16[256,256]{1,0:T(8,12...) custom-call(s32[5]{0:T(128)} %stack.23.place_ref.refs_0_, ...), custom_call_target="tpu_custom_call" | custom-call | flops 14495514624 | bytes 18874368 | tf_op jit(solution)/shard_map/feed/pallas_call | solution.py:734
  144.6 3.2 %collective-permute-done.27 = bf16[4,4,16,4608]{3,2,1,0:T(8,128)(2,1)S(1)} collective-permute-done((bf16[4,4,16,4608]{3,2,1,0:T(8,128)(2,1)}, bf16[4,4,16,4608]{3,2,1,0:T(8,128)(2,1)S(1)}, u32[]{:S(2)}, u32[]{:S(2)}) %collective-permute-start.27) | collective-permute-done | bytes 2359328 | tf_op jit(solution)/shard_map/ppermute | solution.py:105
  147.7 2.3 add_convert_fusion.1
  150.6 1.1 collective-permute-start.31
  151.8 1.9 collective-permute-start.32
  154.3 17.6 %long_backward.1 = (bf16[4,256,512]{2,1,0:T(8,128)(2,1)}, bf16[4,256,512]{2,1,0:T(8,128)(2,1)}, f32[512,256]{1,0:T(8,128)}, f32[2,256,256]{2,1,0:T(8,128)}, f32[...) custom-call(s32[5]{0:T(128)} %stack.23.place_ref.refs_0_, bf16[4,16,4608]{2,1,0:T(8,128)(2,1)} %copy-done.11, ...), custom_call_target="tpu_custom_call" | custom-call | flops 10737418240 | bytes 16777216 | tf_op jit(solution)/shard_map/long_backward/pallas_call | solution.py:878
  172.0 7.6 %collective-permute-done.32 = bf16[4,16,4608]{2,1,0:T(8,128)(2,1)S(1)} collective-permute-done((bf16[4,16,4608]{2,1,0:T(8,128)(2,1)S(1)}, bf16[4,16,4608]{2,1,0:T(8,128)(2,1)S(1)}, u32[]{:S(2)}, u32[]{:S(2)}) %collective-permute-start.32) | collective-permute-done | bytes 589856 | tf_op jit(solution)/shard_map/ppermute | solution.py:112
  179.8 0.8 collective-permute-start.45
  180.6 1.8 collective-permute-start.46
  182.4 1.2 collective-permute-start.47
  185.0 19.3 %long_backward_final.1 = (bf16[4,256,512]{2,1,0:T(8,128)(2,1)}, bf16[4,256,512]{2,1,0:T(8,128)(2,1)}, f32[512,256]{1,0:T(8,128)}, f32[2,256,256]{2,1,0:T(8,128)}...) custom-call(s32[5]{0:T(128)} %stack.23.place_ref.refs_0_, bf16[4,256,512]{2,1,0:T(8,128)(2,1)} %copy-done.3, ...), custom_call_target="tpu_custom_call" | custom-call | flops 10737418240 | bytes 16777216 | tf_op jit(solution)/shard_map/long_backward_final/pallas_call | solution.py:878
  204.4 1.1 fusion.22
  206.2 1.1 collective-permute-done.33
  207.8 2.2 fusion.34
  210.0 1.0 collective-permute-start.35
  211.0 1.0 collective-permute-start.36
  212.0 1.7 collective-permute-start.37
  213.8 22.1 %short_backward.1 = (bf16[768,512]{1,0:T(8,128)(2,1)}, bf16[4,4,16,1664]{3,2,1,0:T(8,128)(2,1)}, bf16[4,4,16,1664]{3,2,1,0:T(8,128)(2,1)}) custom-call(s32[5]{0:T(128)} %stack.23.place_ref.refs_0_, bf16[256,512]{1,0:T(8,128)(2,1)} %get-tuple-element.132.refs_1_, bf16[256,512]{1,0:T(8,128)(2,1)} %get-tuple-element.131.refs_2_, ...), custom_call_target="tpu_custom_call" | custom-call | flops 7247757312 | bytes 18874368 | tf_op jit(solution)/shard_map/short_backward/pallas_call | solution.py:1012
  237.5 1.6 fusion.59
  239.1 1.5 add_convert_fusion.11
  241.2 1.1 collective-permute-start.40
  242.3 1.9 collective-permute-start.41
  244.4 3.9 %collective-permute-done.39 = bf16[4,16,1664]{2,1,0:T(8,128)(2,1)S(1)} collective-permute-done((bf16[4,16,1664]{2,1,0:T(8,128)(2,1)S(1)}, bf16[4,16,1664]{2,1,0:T(8,128)(2,1)S(1)}, u32[]{:S(2)}, u32[]{:S(2)}) %collective-permute-start.39) | collective-permute-done | bytes 213024 | tf_op jit(solution)/shard_map/ppermute | solution.py:112
  248.4 0.9 collective-permute-done.40
  249.3 4.8 %collective-permute-done.41 = bf16[4,16,1664]{2,1,0:T(8,128)(2,1)S(1)} collective-permute-done((bf16[4,16,1664]{2,1,0:T(8,128)(2,1)S(1)}, bf16[4,16,1664]{2,1,0:T(8,128)(2,1)S(1)}, u32[]{:S(2)}, u32[]{:S(2)}) %collective-permute-start.41) | collective-permute-done | bytes 213024 | tf_op jit(solution)/shard_map/ppermute | solution.py:112
  254.2 0.8 collective-permute-start.42
  255.0 1.9 collective-permute-start.43
  256.9 1.5 collective-permute-start.44
  258.4 1.0 maximum_bitcast_fusion
  259.4 1.0 collective-permute-done.42
  260.4 1.3 collective-permute-done.43
  262.4 0.8 slice_reduce_fusion
  (164 shorter events, 22.3 us)
Async XLA Ops:
  2.3 7.5 %collective-permute-start = (bf16[16,1664]{1,0:T(8,128)(2,1)}, bf16[16,1664]{1,0:T(8,128)(2,1)S(1)}, u32[]{:S(2)}, u32[]{:S(2)}) collective-permute-start(bf16[16,1664]{1,0:T(8,128)(2,1)} %pack_first.1.refs_0_), channel_id=1, source_target_pairs={{0,8},{2,10},{4,12},{6,14},{8,16},{10,18},{12,20},{14,22},{16,24},... | collective-permute-start | bytes 159752 | tf_op jit(solution)/shard_map/ppermute | solution.py:102
  5.3 6.6 %collective-permute-start.1 = (bf16[16,1664]{1,0:T(8,128)(2,1)}, bf16[16,1664]{1,0:T(8,128)(2,1)S(1)}, u32[]{:S(2)}, u32[]{:S(2)}) collective-permute-start(bf16[16,1664]{1,0:T(8,128)(2,1)} %pack_first.1.refs_0_), channel_id=1, source_target_pairs={{0,16},{2,18},{4,20},{6,22},{8,24},{10,26},{12,28},{14,30},{16,0},... | collective-permute-start | bytes 159752 | tf_op jit(solution)/shard_map/ppermute | solution.py:102
  7.9 4.5 %collective-permute-start.2 = (bf16[16,1664]{1,0:T(8,128)(2,1)}, bf16[16,1664]{1,0:T(8,128)(2,1)S(1)}, u32[]{:S(2)}, u32[]{:S(2)}) collective-permute-start(bf16[16,1664]{1,0:T(8,128)(2,1)} %pack_first.1.refs_0_), channel_id=1, source_target_pairs={{0,24},{2,26},{4,28},{6,30},{8,0},{10,2},{12,4},{14,6},{16,8},{18,... | collective-permute-start | bytes 159752 | tf_op jit(solution)/shard_map/ppermute | solution.py:102
  14.8 9.2 %collective-permute-start.3 = (bf16[4,16,1664]{2,1,0:T(8,128)(2,1)}, bf16[4,16,1664]{2,1,0:T(8,128)(2,1)S(1)}, u32[]{:S(2)}, u32[]{:S(2)}) collective-permute-start(bf16[4,16,1664]{2,1,0:T(8,128)(2,1)} %stack_blocks.3.refs_0_), channel_id=1, source_target_pairs={{0,1},{1,0},{2,3},{3,2},{4,5},{5,4},{6,7},{7,6},{8,9},{9,8},{10,11... | collective-permute-start | bytes 638984 | tf_op jit(solution)/shard_map/ppermute | solution.py:112
  16.7 26.1 %copy-start.7 = (bf16[4,16,1664]{2,1,0:T(8,128)(2,1)S(1)}, bf16[4,16,1664]{2,1,0:T(8,128)(2,1)}, u32[]{:S(2)}) copy-start(bf16[4,16,1664]{2,1,0:T(8,128)(2,1)} %stack_blocks.3.refs_0_) | copy-start | bytes 638980
  16.7 27.2 %copy-start.32 = (s32[1,1024]{1,0:T(1,128)S(1)}, s32[1,1024]{1,0:T(1,128)}, u32[]{:S(2)}) copy-start(s32[1,1024]{1,0:T(1,128)} %param.17) | copy-start | bytes 12292
  18.4 13.7 %collective-permute-start.6 = (bf16[256,512]{1,0:T(8,128)(2,1)}, bf16[256,512]{1,0:T(8,128)(2,1)S(1)}, u32[]{:S(2)}, u32[]{:S(2)}) collective-permute-start(bf16[256,512]{1,0:T(8,128)(2,1)} %pack_rows.1.refs_3_), channel_id=1, source_target_pairs={{0,8},{2,10},{4,12},{6,14},{8,16},{10,18},{12,20},{14,22},{16,24},... | collective-permute-start | bytes 786440 | tf_op jit(solution)/shard_map/ppermute | solution.py:102
  18.8 18.9 %collective-permute-start.7 = (bf16[256,512]{1,0:T(8,128)(2,1)}, bf16[256,512]{1,0:T(8,128)(2,1)S(1)}, u32[]{:S(2)}, u32[]{:S(2)}) collective-permute-start(bf16[256,512]{1,0:T(8,128)(2,1)} %pack_rows.1.refs_3_), channel_id=1, source_target_pairs={{0,16},{2,18},{4,20},{6,22},{8,24},{10,26},{12,28},{14,30},{16,0},... | collective-permute-start | bytes 786440 | tf_op jit(solution)/shard_map/ppermute | solution.py:102
  21.4 16.3 %collective-permute-start.8 = (bf16[256,512]{1,0:T(8,128)(2,1)}, bf16[256,512]{1,0:T(8,128)(2,1)S(1)}, u32[]{:S(2)}, u32[]{:S(2)}) collective-permute-start(bf16[256,512]{1,0:T(8,128)(2,1)} %pack_rows.1.refs_3_), channel_id=1, source_target_pairs={{0,24},{2,26},{4,28},{6,30},{8,0},{10,2},{12,4},{14,6},{16,8},{18,... | collective-permute-start | bytes 786440 | tf_op jit(solution)/shard_map/ppermute | solution.py:102
  22.5 6.8 %collective-permute-start.4 = (bf16[4,16,1664]{2,1,0:T(8,128)(2,1)}, bf16[4,16,1664]{2,1,0:T(8,128)(2,1)S(1)}, u32[]{:S(2)}, u32[]{:S(2)}) collective-permute-start(bf16[4,16,1664]{2,1,0:T(8,128)(2,1)} %stack_blocks.3.refs_0_), channel_id=1, source_target_pairs={{0,4},{1,5},{2,6},{3,7},{4,0},{5,1},{6,2},{7,3},{8,12},{9,13},{10,... | collective-permute-start | bytes 638984 | tf_op jit(solution)/shard_map/ppermute | solution.py:112
  24.0 13.8 %copy-start.20 = (bf16[4,16,1664]{2,1,0:T(8,128)(2,1)}, bf16[4,16,1664]{2,1,0:T(8,128)(2,1)S(1)}, u32[]{:S(2)}) copy-start(bf16[4,16,1664]{2,1,0:T(8,128)(2,1)S(1)} %collective-permute-done.3.refs_0_.refs_1_) | copy-start | bytes 638980
  24.0 8.1 %collective-permute-start.5 = (bf16[4,16,1664]{2,1,0:T(8,128)(2,1)}, bf16[4,16,1664]{2,1,0:T(8,128)(2,1)S(1)}, u32[]{:S(2)}, u32[]{:S(2)}) collective-permute-start(bf16[4,16,1664]{2,1,0:T(8,128)(2,1)} %stack_blocks.3.refs_0_), channel_id=1, source_target_pairs={{0,5},{1,4},{2,7},{3,6},{4,1},{5,0},{6,3},{7,2},{8,13},{9,12},{10,... | collective-permute-start | bytes 638984 | tf_op jit(solution)/shard_map/ppermute | solution.py:112
  29.2 8.5 %copy-start.21 = (bf16[4,16,1664]{2,1,0:T(8,128)(2,1)}, bf16[4,16,1664]{2,1,0:T(8,128)(2,1)S(1)}, u32[]{:S(2)}) copy-start(bf16[4,16,1664]{2,1,0:T(8,128)(2,1)S(1)} %collective-permute-done.4.refs_1_.refs_2_) | copy-start | bytes 638980
  32.1 5.7 %copy-start.22 = (bf16[4,16,1664]{2,1,0:T(8,128)(2,1)}, bf16[4,16,1664]{2,1,0:T(8,128)(2,1)S(1)}, u32[]{:S(2)}) copy-start(bf16[4,16,1664]{2,1,0:T(8,128)(2,1)S(1)} %collective-permute-done.5.refs_2_.refs_3_) | copy-start | bytes 638980
  32.1 5.7 %copy-start.17 = (bf16[256,512]{1,0:T(8,128)(2,1)}, bf16[256,512]{1,0:T(8,128)(2,1)S(1)}, u32[]{:S(2)}) copy-start(bf16[256,512]{1,0:T(8,128)(2,1)S(1)} %collective-permute-done.6.refs_4_) | copy-start | bytes 786436
  41.4 38.1 %collective-permute-start.17 = (bf16[4,256,512]{2,1,0:T(8,128)(2,1)}, bf16[4,256,512]{2,1,0:T(8,128)(2,1)S(1)}, u32[]{:S(2)}, u32[]{:S(2)}) collective-permute-start(bf16[4,256,512]{2,1,0:T(8,128)(2,1)} %stack_blocks.4.refs_0_.refs_2_), channel_id=1, source_target_pairs={{0,4},{2,6},{4,0},{6,2},{8,12},{10,14},{12,8},{14,10},{16,20},{18,... | collective-permute-start | bytes 3145736 | tf_op jit(solution)/shard_map/ppermute | solution.py:105
  42.9 3.2 %collective-permute-start.9 = (bf16[4,16,1664]{2,1,0:T(8,128)(2,1)S(1)}, bf16[4,16,1664]{2,1,0:T(8,128)(2,1)S(1)}, u32[]{:S(2)}, u32[]{:S(2)}) collective-permute-start(bf16[4,16,1664]{2,1,0:T(8,128)(2,1)S(1)} %copy-done.7), channel_id=1, source_target_pairs={{0,2},{2,0},{4,6},{6,4},{8,10},{10,8},{12,14},{14,12},{16,18},{18,... | collective-permute-start | bytes 638984 | tf_op jit(solution)/shard_map/ppermute | solution.py:105
  42.9 3.2 %collective-permute-start.10 = (bf16[4,16,1664]{2,1,0:T(8,128)(2,1)}, bf16[4,16,1664]{2,1,0:T(8,128)(2,1)S(1)}, u32[]{:S(2)}, u32[]{:S(2)}) collective-permute-start(bf16[4,16,1664]{2,1,0:T(8,128)(2,1)} %copy-done.20), channel_id=1, source_target_pairs={{0,2},{2,0},{4,6},{6,4},{8,10},{10,8},{12,14},{14,12},{16,18},{18,... | collective-permute-start | bytes 638984 | tf_op jit(solution)/shard_map/ppermute | solution.py:105
  43.4 2.7 %collective-permute-start.11 = (bf16[4,16,1664]{2,1,0:T(8,128)(2,1)}, bf16[4,16,1664]{2,1,0:T(8,128)(2,1)S(1)}, u32[]{:S(2)}, u32[]{:S(2)}) collective-permute-start(bf16[4,16,1664]{2,1,0:T(8,128)(2,1)} %copy-done.21), channel_id=1, source_target_pairs={{0,2},{2,0},{4,6},{6,4},{8,10},{10,8},{12,14},{14,12},{16,18},{18,... | collective-permute-start | bytes 638984 | tf_op jit(solution)/shard_map/ppermute | solution.py:105
  43.4 2.7 %collective-permute-start.12 = (bf16[4,16,1664]{2,1,0:T(8,128)(2,1)}, bf16[4,16,1664]{2,1,0:T(8,128)(2,1)S(1)}, u32[]{:S(2)}, u32[]{:S(2)}) collective-permute-start(bf16[4,16,1664]{2,1,0:T(8,128)(2,1)} %copy-done.22), channel_id=1, source_target_pairs={{0,2},{2,0},{4,6},{6,4},{8,10},{10,8},{12,14},{14,12},{16,18},{18,... | collective-permute-start | bytes 638984 | tf_op jit(solution)/shard_map/ppermute | solution.py:105
  46.0 38.4 %collective-permute-start.16 = (bf16[4,256,512]{2,1,0:T(8,128)(2,1)}, bf16[4,256,512]{2,1,0:T(8,128)(2,1)}, u32[]{:S(2)}, u32[]{:S(2)}) collective-permute-start(bf16[4,256,512]{2,1,0:T(8,128)(2,1)} %stack_blocks.4.refs_0_.refs_2_), channel_id=1, source_target_pairs={{0,2},{2,0},{4,6},{6,4},{8,10},{10,8},{12,14},{14,12},{16,18},{18,... | collective-permute-start | bytes 3145736 | tf_op jit(solution)/shard_map/ppermute | solution.py:105
  56.1 20.6 %collective-permute-start.13 = (bf16[16,4608]{1,0:T(8,128)(2,1)}, bf16[16,4608]{1,0:T(8,128)(2,1)S(1)}, u32[]{:S(2)}, u32[]{:S(2)}) collective-permute-start(bf16[16,4608]{1,0:T(8,128)(2,1)} %pack_second.1.refs_1_), channel_id=1, source_target_pairs={{0,8},{2,10},{4,12},{6,14},{8,16},{10,18},{12,20},{14,22},{16,24},... | collective-permute-start | bytes 442376 | tf_op jit(solution)/shard_map/ppermute | solution.py:102
  61.5 15.3 %collective-permute-start.14 = (bf16[16,4608]{1,0:T(8,128)(2,1)}, bf16[16,4608]{1,0:T(8,128)(2,1)S(1)}, u32[]{:S(2)}, u32[]{:S(2)}) collective-permute-start(bf16[16,4608]{1,0:T(8,128)(2,1)} %pack_second.1.refs_1_), channel_id=1, source_target_pairs={{0,16},{2,18},{4,20},{6,22},{8,24},{10,26},{12,28},{14,30},{16,0},... | collective-permute-start | bytes 442376 | tf_op jit(solution)/shard_map/ppermute | solution.py:102
  62.6 14.2 %collective-permute-start.15 = (bf16[16,4608]{1,0:T(8,128)(2,1)}, bf16[16,4608]{1,0:T(8,128)(2,1)S(1)}, u32[]{:S(2)}, u32[]{:S(2)}) collective-permute-start(bf16[16,4608]{1,0:T(8,128)(2,1)} %pack_second.1.refs_1_), channel_id=1, source_target_pairs={{0,24},{2,26},{4,28},{6,30},{8,0},{10,2},{12,4},{14,6},{16,8},{18,... | collective-permute-start | bytes 442376 | tf_op jit(solution)/shard_map/ppermute | solution.py:102
  80.5 4.0 %collective-permute-start.18 = (bf16[4,256,512]{2,1,0:T(8,128)(2,1)}, bf16[4,256,512]{2,1,0:T(8,128)(2,1)S(1)}, u32[]{:S(2)}, u32[]{:S(2)}) collective-permute-start(bf16[4,256,512]{2,1,0:T(8,128)(2,1)} %tie.2.refs_4_), channel_id=1, source_target_pairs={{0,2},{2,0},{4,6},{6,4},{8,10},{10,8},{12,14},{14,12},{16,18},{18,... | collective-permute-start | bytes 3145736 | tf_op jit(solution)/shard_map/ppermute | solution.py:105
  80.9 30.1 %collective-permute-start.20 = (bf16[4,16,4608]{2,1,0:T(8,128)(2,1)S(1)}, bf16[4,16,4608]{2,1,0:T(8,128)(2,1)S(1)}, u32[]{:S(2)}, u32[]{:S(2)}) collective-permute-start(bf16[4,16,4608]{2,1,0:T(8,128)(2,1)S(1)} %copy-done.2), channel_id=1, source_target_pairs={{0,1},{1,0},{2,3},{3,2},{4,5},{5,4},{6,7},{7,6},{8,9},{9,8},{10,11... | collective-permute-start | bytes 1769480 | tf_op jit(solution)/shard_map/ppermute | solution.py:112
  81.5 29.6 %collective-permute-start.21 = (bf16[4,16,4608]{2,1,0:T(8,128)(2,1)S(1)}, bf16[4,16,4608]{2,1,0:T(8,128)(2,1)S(1)}, u32[]{:S(2)}, u32[]{:S(2)}) collective-permute-start(bf16[4,16,4608]{2,1,0:T(8,128)(2,1)S(1)} %copy-done.2), channel_id=1, source_target_pairs={{0,4},{1,5},{2,6},{3,7},{4,0},{5,1},{6,2},{7,3},{8,12},{9,13},{10,... | collective-permute-start | bytes 1769480 | tf_op jit(solution)/shard_map/ppermute | solution.py:112
  82.6 28.5 %collective-permute-start.22 = (bf16[4,16,4608]{2,1,0:T(8,128)(2,1)S(1)}, bf16[4,16,4608]{2,1,0:T(8,128)(2,1)S(1)}, u32[]{:S(2)}, u32[]{:S(2)}) collective-permute-start(bf16[4,16,4608]{2,1,0:T(8,128)(2,1)S(1)} %copy-done.2), channel_id=1, source_target_pairs={{0,5},{1,4},{2,7},{3,6},{4,1},{5,0},{6,3},{7,2},{8,13},{9,12},{10,... | collective-permute-start | bytes 1769480 | tf_op jit(solution)/shard_map/ppermute | solution.py:112
  84.4 29.9 %collective-permute-start.23 = (bf16[4,16,4608]{2,1,0:T(8,128)(2,1)S(1)}, bf16[4,16,4608]{2,1,0:T(8,128)(2,1)S(1)}, u32[]{:S(2)}, u32[]{:S(2)}) collective-permute-start(bf16[4,16,4608]{2,1,0:T(8,128)(2,1)S(1)} %copy-done.2), channel_id=1, source_target_pairs={{0,2},{2,0},{4,6},{6,4},{8,10},{10,8},{12,14},{14,12},{16,18},{18,... | collective-permute-start | bytes 1769480 | tf_op jit(solution)/shard_map/ppermute | solution.py:105
  112.3 4.2 %collective-permute-start.24 = (bf16[4,16,4608]{2,1,0:T(8,128)(2,1)}, bf16[4,16,4608]{2,1,0:T(8,128)(2,1)S(1)}, u32[]{:S(2)}, u32[]{:S(2)}) collective-permute-start(bf16[4,16,4608]{2,1,0:T(8,128)(2,1)} %get-tuple-element.79.refs_1_), channel_id=1, source_target_pairs={{0,2},{2,0},{4,6},{6,4},{8,10},{10,8},{12,14},{14,12},{16,18},{18,... | collective-permute-start | bytes 1769480 | tf_op jit(solution)/shard_map/ppermute | solution.py:105
  112.8 3.7 %collective-permute-start.25 = (bf16[4,16,4608]{2,1,0:T(8,128)(2,1)}, bf16[4,16,4608]{2,1,0:T(8,128)(2,1)S(1)}, u32[]{:S(2)}, u32[]{:S(2)}) collective-permute-start(bf16[4,16,4608]{2,1,0:T(8,128)(2,1)} %get-tuple-element.80.refs_2_), channel_id=1, source_target_pairs={{0,2},{2,0},{4,6},{6,4},{8,10},{10,8},{12,14},{14,12},{16,18},{18,... | collective-permute-start | bytes 1769480 | tf_op jit(solution)/shard_map/ppermute | solution.py:105
  112.8 3.7 %collective-permute-start.26 = (bf16[4,16,4608]{2,1,0:T(8,128)(2,1)}, bf16[4,16,4608]{2,1,0:T(8,128)(2,1)S(1)}, u32[]{:S(2)}, u32[]{:S(2)}) collective-permute-start(bf16[4,16,4608]{2,1,0:T(8,128)(2,1)} %get-tuple-element.81.refs_3_), channel_id=1, source_target_pairs={{0,2},{2,0},{4,6},{6,4},{8,10},{10,8},{12,14},{14,12},{16,18},{18,... | collective-permute-start | bytes 1769480 | tf_op jit(solution)/shard_map/ppermute | solution.py:105
  113.3 3.2 %collective-permute-start.19 = (bf16[256,256]{1,0:T(8,128)(2,1)}, bf16[256,256]{1,0:T(8,128)(2,1)S(1)}, u32[]{:S(2)}, u32[]{:S(2)}) collective-permute-start(bf16[256,256]{1,0:T(8,128)(2,1)} %get-tuple-element.76), channel_id=1, source_target_pairs={{0,2},{2,0},{4,6},{6,4},{8,10},{10,8},{12,14},{14,12},{16,18},{18,... | collective-permute-start | bytes 393224 | tf_op jit(solution)/shard_map/ppermute | solution.py:105
  117.8 25.6 %copy-start = (bf16[1,1024,512]{2,1,0:T(8,128)(2,1)S(1)}, bf16[1,1024,512]{2,1,0:T(8,128)(2,1)}, u32[]{:S(2)}) copy-start(bf16[1,1024,512]{2,1,0:T(8,128)(2,1)} %param.16) | copy-start | bytes 3145732
  143.0 4.7 %collective-permute-start.27 = (bf16[4,4,16,4608]{3,2,1,0:T(8,128)(2,1)}, bf16[4,4,16,4608]{3,2,1,0:T(8,128)(2,1)S(1)}, u32[]{:S(2)}, u32[]{:S(2)}) collective-permute-start(bf16[4,4,16,4608]{3,2,1,0:T(8,128)(2,1)} %get-tuple-element.85), channel_id=1, source_target_pairs={{0,2},{2,0},{4,6},{6,4},{8,10},{10,8},{12,14},{14,12},{16,18},{18,... | collective-permute-start | bytes 7077896 | tf_op jit(solution)/shard_map/ppermute | solution.py:105
  144.4 9.2 %collective-permute-start.28 = (bf16[256,256]{1,0:T(8,128)(2,1)}, bf16[256,256]{1,0:T(8,128)(2,1)S(1)}, u32[]{:S(2)}, u32[]{:S(2)}) collective-permute-start(bf16[256,256]{1,0:T(8,128)(2,1)} %get-tuple-element.89), channel_id=1, source_target_pairs={{0,2},{2,0},{4,6},{6,4},{8,10},{10,8},{12,14},{14,12},{16,18},{18,... | collective-permute-start | bytes 393224 | tf_op jit(solution)/shard_map/ppermute | solution.py:105
  150.0 3.6 %copy-start.9 = (bf16[4,16,4608]{2,1,0:T(8,128)(2,1)}, bf16[4,16,4608]{2,1,0:T(8,128)(2,1)S(1)}, u32[]{:S(2)}) copy-start(bf16[4,16,4608]{2,1,0:T(8,128)(2,1)S(1)} %get-tuple-element.127.refs_3_) | copy-start | bytes 1769476
  150.1 21.9 %collective-permute-start.30 = (bf16[4,16,4608]{2,1,0:T(8,128)(2,1)S(1)}, bf16[4,16,4608]{2,1,0:T(8,128)(2,1)S(1)}, u32[]{:S(2)}, u32[]{:S(2)}) collective-permute-start(bf16[4,16,4608]{2,1,0:T(8,128)(2,1)S(1)} %get-tuple-element.129.refs_1_), channel_id=1, source_target_pairs={{0,1},{1,0},{2,3},{3,2},{4,5},{5,4},{6,7},{7,6},{8,9},{9,8},{10,11... | collective-permute-start | bytes 1769480 | tf_op jit(solution)/shard_map/ppermute | solution.py:112
  150.6 21.3 %collective-permute-start.31 = (bf16[4,16,4608]{2,1,0:T(8,128)(2,1)S(1)}, bf16[4,16,4608]{2,1,0:T(8,128)(2,1)S(1)}, u32[]{:S(2)}, u32[]{:S(2)}) collective-permute-start(bf16[4,16,4608]{2,1,0:T(8,128)(2,1)S(1)} %get-tuple-element.128.refs_2_), channel_id=1, source_target_pairs={{0,4},{1,5},{2,6},{3,7},{4,0},{5,1},{6,2},{7,3},{8,12},{9,13},{10,... | collective-permute-start | bytes 1769480 | tf_op jit(solution)/shard_map/ppermute | solution.py:112
  151.8 27.8 %collective-permute-start.32 = (bf16[4,16,4608]{2,1,0:T(8,128)(2,1)S(1)}, bf16[4,16,4608]{2,1,0:T(8,128)(2,1)S(1)}, u32[]{:S(2)}, u32[]{:S(2)}) collective-permute-start(bf16[4,16,4608]{2,1,0:T(8,128)(2,1)S(1)} %get-tuple-element.127.refs_3_), channel_id=1, source_target_pairs={{0,5},{1,4},{2,7},{3,6},{4,1},{5,0},{6,3},{7,2},{8,13},{9,12},{10,... | collective-permute-start | bytes 1769480 | tf_op jit(solution)/shard_map/ppermute | solution.py:112
  171.9 11.8 %copy-start.4 = (bf16[4,256,512]{2,1,0:T(8,128)(2,1)S(1)}, bf16[4,256,512]{2,1,0:T(8,128)(2,1)}, u32[]{:S(2)}) copy-start(bf16[4,256,512]{2,1,0:T(8,128)(2,1)} %get-tuple-element.92) | copy-start | bytes 3145732
  171.9 11.8 %collective-permute-start.29 = (bf16[4,256,512]{2,1,0:T(8,128)(2,1)}, bf16[4,256,512]{2,1,0:T(8,128)(2,1)S(1)}, u32[]{:S(2)}, u32[]{:S(2)}) collective-permute-start(bf16[4,256,512]{2,1,0:T(8,128)(2,1)} %get-tuple-element.93), channel_id=1, source_target_pairs={{0,2},{2,0},{4,6},{6,4},{8,10},{10,8},{12,14},{14,12},{16,18},{18,... | collective-permute-start | bytes 3145736 | tf_op jit(solution)/shard_map/ppermute | solution.py:105
  179.5 4.1 %copy-start.15 = (bf16[4,16,4608]{2,1,0:T(8,128)(2,1)}, bf16[4,16,4608]{2,1,0:T(8,128)(2,1)S(1)}, u32[]{:S(2)}) copy-start(bf16[4,16,4608]{2,1,0:T(8,128)(2,1)S(1)} %collective-permute-done.32) | copy-start | bytes 1769476
  179.8 4.9 %copy-start.23 = (bf16[16,4608]{1,0:T(8,128)(2,1)}, bf16[16,4608]{1,0:T(8,128)(2,1)S(1)}, u32[]{:S(2)}) copy-start(bf16[16,4608]{1,0:T(8,128)(2,1)S(1)} %get-tuple-element.133.refs_4_) | copy-start | bytes 442372
  179.8 4.9 %copy-start.24 = (bf16[16,4608]{1,0:T(8,128)(2,1)}, bf16[16,4608]{1,0:T(8,128)(2,1)S(1)}, u32[]{:S(2)}) copy-start(bf16[16,4608]{1,0:T(8,128)(2,1)S(1)} %get-tuple-element.134.refs_3_) | copy-start | bytes 442372
  179.8 4.9 %copy-start.25 = (bf16[16,4608]{1,0:T(8,128)(2,1)}, bf16[16,4608]{1,0:T(8,128)(2,1)S(1)}, u32[]{:S(2)}) copy-start(bf16[16,4608]{1,0:T(8,128)(2,1)S(1)} %get-tuple-element.135.refs_2_) | copy-start | bytes 442372
  179.8 24.6 %collective-permute-start.45 = (bf16[16,4608]{1,0:T(8,128)(2,1)S(1)}, bf16[16,4608]{1,0:T(8,128)(2,1)S(1)}, u32[]{:S(2)}, u32[]{:S(2)}) collective-permute-start(bf16[16,4608]{1,0:T(8,128)(2,1)S(1)} %get-tuple-element.135.refs_2_), channel_id=1, source_target_pairs={{0,8},{2,10},{4,12},{6,14},{8,16},{10,18},{12,20},{14,22},{16,24},... | collective-permute-start | bytes 442376 | tf_op jit(solution)/shard_map/ppermute | solution.py:102
  180.6 23.8 %collective-permute-start.46 = (bf16[16,4608]{1,0:T(8,128)(2,1)S(1)}, bf16[16,4608]{1,0:T(8,128)(2,1)S(1)}, u32[]{:S(2)}, u32[]{:S(2)}) collective-permute-start(bf16[16,4608]{1,0:T(8,128)(2,1)S(1)} %get-tuple-element.134.refs_3_), channel_id=1, source_target_pairs={{0,16},{2,18},{4,20},{6,22},{8,24},{10,26},{12,28},{14,30},{16,0},... | collective-permute-start | bytes 442376 | tf_op jit(solution)/shard_map/ppermute | solution.py:102
  182.4 22.0 %collective-permute-start.47 = (bf16[16,4608]{1,0:T(8,128)(2,1)S(1)}, bf16[16,4608]{1,0:T(8,128)(2,1)}, u32[]{:S(2)}, u32[]{:S(2)}) collective-permute-start(bf16[16,4608]{1,0:T(8,128)(2,1)S(1)} %get-tuple-element.133.refs_4_), channel_id=1, source_target_pairs={{0,24},{2,26},{4,28},{6,30},{8,0},{10,2},{12,4},{14,6},{16,8},{18,... | collective-permute-start | bytes 442376 | tf_op jit(solution)/shard_map/ppermute | solution.py:102
  184.0 23.8 %collective-permute-start.34 = (bf16[4,256,512]{2,1,0:T(8,128)(2,1)S(1)}, bf16[4,256,512]{2,1,0:T(8,128)(2,1)S(1)}, u32[]{:S(2)}, u32[]{:S(2)}) collective-permute-start(bf16[4,256,512]{2,1,0:T(8,128)(2,1)S(1)} %add_convert_fusion.refs_1_), channel_id=1, source_target_pairs={{0,4},{2,6},{4,0},{6,2},{8,12},{10,14},{12,8},{14,10},{16,20},{18,... | collective-permute-start | bytes 3145736 | tf_op jit(solution)/shard_map/ppermute | solution.py:105
  204.3 2.9 %collective-permute-start.33 = (bf16[4,256,512]{2,1,0:T(8,128)(2,1)}, bf16[4,256,512]{2,1,0:T(8,128)(2,1)S(1)}, u32[]{:S(2)}, u32[]{:S(2)}) collective-permute-start(bf16[4,256,512]{2,1,0:T(8,128)(2,1)} %get-tuple-element.99), channel_id=1, source_target_pairs={{0,2},{2,0},{4,6},{6,4},{8,10},{10,8},{12,14},{14,12},{16,18},{18,... | collective-permute-start | bytes 3145736 | tf_op jit(solution)/shard_map/ppermute | solution.py:105
  210.0 27.4 %collective-permute-start.35 = (bf16[256,512]{1,0:T(8,128)(2,1)}, bf16[256,512]{1,0:T(8,128)(2,1)}, u32[]{:S(2)}, u32[]{:S(2)}) collective-permute-start(bf16[256,512]{1,0:T(8,128)(2,1)} %get-tuple-element.132.refs_1_), channel_id=1, source_target_pairs={{0,24},{2,26},{4,28},{6,30},{8,0},{10,2},{12,4},{14,6},{16,8},{18,... | collective-permute-start | bytes 786440 | tf_op jit(solution)/shard_map/ppermute | solution.py:102
  211.0 26.4 %collective-permute-start.36 = (bf16[256,512]{1,0:T(8,128)(2,1)}, bf16[256,512]{1,0:T(8,128)(2,1)}, u32[]{:S(2)}, u32[]{:S(2)}) collective-permute-start(bf16[256,512]{1,0:T(8,128)(2,1)} %get-tuple-element.131.refs_2_), channel_id=1, source_target_pairs={{0,16},{2,18},{4,20},{6,22},{8,24},{10,26},{12,28},{14,30},{16,0},... | collective-permute-start | bytes 786440 | tf_op jit(solution)/shard_map/ppermute | solution.py:102
  212.0 25.4 %collective-permute-start.37 = (bf16[256,512]{1,0:T(8,128)(2,1)}, bf16[256,512]{1,0:T(8,128)(2,1)}, u32[]{:S(2)}, u32[]{:S(2)}) collective-permute-start(bf16[256,512]{1,0:T(8,128)(2,1)} %get-tuple-element.130.refs_3_), channel_id=1, source_target_pairs={{0,8},{2,10},{4,12},{6,14},{8,16},{10,18},{12,20},{14,22},{16,24},... | collective-permute-start | bytes 786440 | tf_op jit(solution)/shard_map/ppermute | solution.py:102
  213.8 23.7 %copy-start.1 = (bf16[1,1024,512]{2,1,0:T(8,128)(2,1)S(1)}, bf16[1,1024,512]{2,1,0:T(8,128)(2,1)}, u32[]{:S(2)}) copy-start(bf16[1,1024,512]{2,1,0:T(8,128)(2,1)} %param.16) | copy-start | bytes 3145732
  235.9 3.2 %collective-permute-start.38 = (bf16[4,4,16,1664]{3,2,1,0:T(8,128)(2,1)}, bf16[4,4,16,1664]{3,2,1,0:T(8,128)(2,1)}, u32[]{:S(2)}, u32[]{:S(2)}) collective-permute-start(bf16[4,4,16,1664]{3,2,1,0:T(8,128)(2,1)} %get-tuple-element.114), channel_id=1, source_target_pairs={{0,2},{2,0},{4,6},{6,4},{8,10},{10,8},{12,14},{14,12},{16,18},{18,... | collective-permute-start | bytes 2555912 | tf_op jit(solution)/shard_map/ppermute | solution.py:105
  237.4 6.8 %copy-start.16 = (f32[256,512]{1,0:T(8,128)S(1)}, f32[256,512]{1,0:T(8,128)}, u32[]{:S(2)}) copy-start(f32[256,512]{1,0:T(8,128)} %get-tuple-element.83) | copy-start | bytes 1572868
  239.1 19.2 %copy-start.8 = (bf16[768,512]{1,0:T(8,128)(2,1)S(1)}, bf16[768,512]{1,0:T(8,128)(2,1)}, u32[]{:S(2)}) copy-start(bf16[768,512]{1,0:T(8,128)(2,1)} %get-tuple-element.112) | copy-start | bytes 2359300
  240.7 7.7 %collective-permute-start.39 = (bf16[4,16,1664]{2,1,0:T(8,128)(2,1)S(1)}, bf16[4,16,1664]{2,1,0:T(8,128)(2,1)S(1)}, u32[]{:S(2)}, u32[]{:S(2)}) collective-permute-start(bf16[4,16,1664]{2,1,0:T(8,128)(2,1)S(1)} %get-tuple-element.139), channel_id=1, source_target_pairs={{0,1},{1,0},{2,3},{3,2},{4,5},{5,4},{6,7},{7,6},{8,9},{9,8},{10,11... | collective-permute-start | bytes 638984 | tf_op jit(solution)/shard_map/ppermute | solution.py:112
  241.2 8.1 %collective-permute-start.40 = (bf16[4,16,1664]{2,1,0:T(8,128)(2,1)S(1)}, bf16[4,16,1664]{2,1,0:T(8,128)(2,1)S(1)}, u32[]{:S(2)}, u32[]{:S(2)}) collective-permute-start(bf16[4,16,1664]{2,1,0:T(8,128)(2,1)S(1)} %get-tuple-element.138), channel_id=1, source_target_pairs={{0,4},{1,5},{2,6},{3,7},{4,0},{5,1},{6,2},{7,3},{8,12},{9,13},{10,... | collective-permute-start | bytes 638984 | tf_op jit(solution)/shard_map/ppermute | solution.py:112
  242.3 11.8 %collective-permute-start.41 = (bf16[4,16,1664]{2,1,0:T(8,128)(2,1)S(1)}, bf16[4,16,1664]{2,1,0:T(8,128)(2,1)S(1)}, u32[]{:S(2)}, u32[]{:S(2)}) collective-permute-start(bf16[4,16,1664]{2,1,0:T(8,128)(2,1)S(1)} %get-tuple-element.137), channel_id=1, source_target_pairs={{0,5},{1,4},{2,7},{3,6},{4,1},{5,0},{6,3},{7,2},{8,13},{9,12},{10,... | collective-permute-start | bytes 638984 | tf_op jit(solution)/shard_map/ppermute | solution.py:112
  254.2 6.2 %collective-permute-start.42 = (bf16[16,1664]{1,0:T(8,128)(2,1)S(1)}, bf16[16,1664]{1,0:T(8,128)(2,1)S(1)}, u32[]{:S(2)}, u32[]{:S(2)}) collective-permute-start(bf16[16,1664]{1,0:T(8,128)(2,1)S(1)} %get-tuple-element.140), channel_id=1, source_target_pairs={{0,8},{2,10},{4,12},{6,14},{8,16},{10,18},{12,20},{14,22},{16,24},... | collective-permute-start | bytes 159752 | tf_op jit(solution)/shard_map/ppermute | solution.py:102
  255.0 6.7 %collective-permute-start.43 = (bf16[16,1664]{1,0:T(8,128)(2,1)S(1)}, bf16[16,1664]{1,0:T(8,128)(2,1)S(1)}, u32[]{:S(2)}, u32[]{:S(2)}) collective-permute-start(bf16[16,1664]{1,0:T(8,128)(2,1)S(1)} %get-tuple-element.142), channel_id=1, source_target_pairs={{0,16},{2,18},{4,20},{6,22},{8,24},{10,26},{12,28},{14,30},{16,0},... | collective-permute-start | bytes 159752 | tf_op jit(solution)/shard_map/ppermute | solution.py:102
  256.9 4.8 %collective-permute-start.44 = (bf16[16,1664]{1,0:T(8,128)(2,1)S(1)}, bf16[16,1664]{1,0:T(8,128)(2,1)S(1)}, u32[]{:S(2)}, u32[]{:S(2)}) collective-permute-start(bf16[16,1664]{1,0:T(8,128)(2,1)S(1)} %get-tuple-element.141), channel_id=1, source_target_pairs={{0,24},{2,26},{4,28},{6,30},{8,0},{10,2},{12,4},{14,6},{16,8},{18,... | collective-permute-start | bytes 159752 | tf_op jit(solution)/shard_map/ppermute | solution.py:102
  (28 other events, 33.9 us)
where the time goes:
time: 268 us; the launch traced here: 264 us
  Pallas kernels  140 us (52%)
  starting transfers between devices  50.3 us (19%)
  waiting for transfers between devices  43.1 us (16%)
  local copies, waits for them, and re-layouts  18.2 us (7%)
  other arithmetic  11 us (4%)
    pallas_call x2, Pallas kernels, long_backward(): pl.pallas_call(behind(functools.partial(long_backward_kernel, final), len...  36.9 us
    ppermute x18, starting transfers between devices, shift_depth(): return lax.ppermute(block, 'band', pairs)  31 us
    pallas_call x1, Pallas kernels, feed(): pl.pallas_call(functools.partial(feed_kernel, layout), grid_spec=pltpu.Pr...  25.2 us
    ppermute x12, waiting for transfers between devices, shift_plane(): return lax.ppermute(block, ('band', 'batch'), pairs)  24.9 us
    pallas_call x1, Pallas kernels, short_backward(): pl.pallas_call(behind(functools.partial(short_backward_kernel, layout), l...  22.1 us
    pallas_call x1, Pallas kernels, long_forward(): pl.pallas_call(long_forward_kernel, grid=(STEPS + 1,), in_specs=[once((TI...  15 us
    ppermute x12, starting transfers between devices, shift_plane(): return lax.ppermute(block, ('band', 'batch'), pairs)  14.4 us
    pallas_call x1, Pallas kernels, short_forward(): pl.pallas_call(behind(short_forward_kernel, len(deps), False), grid=(HEAD...  12.4 us
  transfers between devices with their start and end apart: 48, of which 16 were waited for; matrix products, arithmetic and copies ran while one was open for 5% of the time, Pallas kernels for 41%

commit v1 on v0

--- a/solution.py
+++ b/solution.py
@@ -156,9 +156,11 @@
                 for kz in range(self.depth):
                     refs[kc][n, kz] = take(self.shard(place, kc, kx, ky, kz, 1))
 
-    def scatter_core(self, parts):
+    def scatter_core(self, parts, deps=()):
         keep, send = parts
         arrived = self.flip(send, 1)
+        if deps:
+            (arrived,) = tie([arrived], deps)
         return [(keep[n].astype(f32) + arrived[n].astype(f32)).astype(bf16) for n in range(len(self.plane))]
 
     def scatter_plane(self, pairs):
@@ -346,7 +348,7 @@
 
     @pl.when(step == 0)
     def _():
-        same = idc_ref[...] == idr_ref[...]
+        same = idc_ref[LONG:, :] == idr_ref[:, LONG:]
         bias_ref[...] = jnp.where(same, 0.0, -1e30)
 
     def first(slot):
@@ -393,7 +395,7 @@
             att_ref[:, low : low + 128] = o_ref[low : low + 128, :].T.astype(bf16)
 
 
-def short_forward(q, k, vt, ids, deps):
+def short_forward(q, k, vt, id_column, id_row, deps):
     count = q.shape[0]
     now = lambda s: (0, jnp.minimum(s, HEADS - 1) // 4)
     before = lambda s: (0, jnp.maximum(s - 1, 0))
@@ -405,8 +407,8 @@
             pl.BlockSpec((count, GROUP), now),
             pl.BlockSpec((count, GROUP), now),
             whole((WIDTH, count)),
-            whole((count, 1)),
-            whole((1, count)),
+            whole(id_column.shape),
+            whole(id_row.shape),
         ],
         out_specs=[
             pl.BlockSpec((count, count), before),
@@ -430,7 +432,7 @@
             flops=12 * count * count * WIDTH, bytes_accessed=12 << 20, transcendentals=HEADS * count * count
         ),
         name="short_forward",
-    )(*deps, q, k, vt, ids[:, None], ids[None, :])
+    )(*deps, q, k, vt, id_column, id_row)
 
 
 CHIPS = 2
@@ -717,10 +719,10 @@
     layout.store_scattered(place_ref, grads, take)
 
 
-def feed(layout, place, rows, ids, upstream, mine, other, short, vectors, hidden_shift, pieces):
+def feed(layout, place, rows, id_column, upstream, mine, other, short, vectors, hidden_shift, pieces):
     count = rows.shape[0]
     grads = layout.scattered_shapes(SECOND)
-    operands = [rows, ids[:, None], upstream, mine, other, short, vectors, hidden_shift]
+    operands = [rows, id_column, upstream, mine, other, short, vectors, hidden_shift]
     shapes = [
         jax.ShapeDtypeStruct((count, WIDTH), bf16),
         jax.ShapeDtypeStruct((LONG, WIDTH), f32),
@@ -759,15 +761,10 @@
 
 
 def long_backward_kernel(
-    final, place_ref, e_ref, k_ref, vt_ref, n1_ref, q_ref, mine_ref, other_ref, o_ref, linv_ref, w_ref, vec_ref,
-    *refs,
+    place_ref, e_ref, k_ref, vt_ref, n1_ref, q_ref, mine_ref, other_ref, o_ref, linv_ref, w_ref, vec_ref,
+    keep0, send0, keep1, send1, gq_ref, gkv_ref, row_ref, side_ref,
+    dq_acc, qblk, dblk, delta, ds_ref, wq, wkv,
 ):
-    if final:
-        dq_in, gkv_in, row_in, side_in, *refs = refs
-    (
-    keep_ref, send_ref, gq_ref, dq_acc, gkv_ref, row_ref, side_ref,
-    qblk, dblk, delta, ds_ref, wq, wkv,
-    ) = refs
     step = pl.program_id(0)
     core = place_ref[1]
 
@@ -777,14 +774,8 @@
         wq[...] = w_ref[:, lanes(0)]
         wkv[:, :GROUP] = w_ref[:, lanes(WIDTH)]
         wkv[:, GROUP:] = w_ref[:, lanes(2 * WIDTH)]
-        if final:
-            dq_acc[...] = dq_in[...]
-            gkv_ref[...] = gkv_in[...]
-            row_ref[...] = row_in[...]
-            side_ref[...] = side_in[...]
-        else:
-            for ref in (dq_acc, gkv_ref, row_ref, side_ref):
-                ref[...] = jnp.zeros_like(ref)
+        for ref in (dq_acc, gkv_ref, row_ref, side_ref):
+            ref[...] = jnp.zeros_like(ref)
         for part in range(PARTS):
             rows = slice(part * CHUNK, (part + 1) * CHUNK)
             turned = (mine_ref, other_ref)[part][...].astype(f32).T
@@ -831,7 +822,7 @@
     gkv_ref[...] += dot(normed, both, 0, 0)
     side_ref[1:2, :] += column_sum(value_grad.astype(f32))
 
-    def put(entire):
+    def put(entire, keep_ref, send_ref):
         low = entire.astype(bf16)
         for chip in range(BACK // TILE):
             base = chip * TILE
@@ -842,14 +833,16 @@
         row_ref[0:1, :] += scales / row_of(vec_ref, V_G1)
         row_ref[1:2, :] += shifts
 
-    if not final:
-        put(through)
-        return
     last = pl.num_programs(0) - 1
-
-    @pl.when(step < last)
-    def _():
-        put(through)
+    half = pl.num_programs(0) // 2
+
+    @pl.when(step < half)
+    def _():
+        put(through, keep1, send1)
+
+    @pl.when((step >= half) & (step < last))
+    def _():
+        put(through, keep0, send0)
 
     @pl.when(step == last)
     def _():
@@ -857,29 +850,32 @@
             [dq_acc[part].T for part in range(PARTS)], axis=0
         ) * (1.0 / math.sqrt(HEAD))
         low = query_grad.astype(bf16)
-        put(jnp.concatenate([through[:TILE, :] + dot(low, wq[...], 1, 1), through[TILE:, :]], axis=0))
+        own = through[:TILE, :] + dot(low, wq[...], 1, 1)
+        put(jnp.concatenate([own, through[TILE:, :]], axis=0), keep0, send0)
         gq_ref[...] = dot(normed[:TILE, :], low, 0, 0)
         side_ref[0:1, :] += column_sum(low.astype(f32))
 
 
-def long_backward(layout, final, place, e, k, vt, normed, q, mine, other, o, linv, weights, vectors, sums, deps):
+def long_backward(layout, place, e, k, vt, normed, q, mine, other, o, linv, weights, vectors, deps):
     tiles = layout.depth * TILE // BACK
-    away = (lambda i: i) if not final else (lambda i: lax.rem(i + 1, tiles))
-    turn = lambda i: away(i) if final else tiles + i
+    near = lambda i: lax.rem(jnp.maximum(i - tiles, 0) + 1, tiles)
+    far = lambda i: jnp.minimum(i, tiles - 1)
+    turn = lambda i: jnp.where(i < tiles, tiles + i, near(i))
+    chips = BACK // TILE
     out = jax.ShapeDtypeStruct((layout.depth, LONG, WIDTH), bf16)
-    out_spec = pl.BlockSpec((BACK // TILE, LONG, WIDTH), lambda i, p: (away(i), 0, 0))
-    sum_shapes = [
-        jax.ShapeDtypeStruct((PARTS, GROUP, CHUNK), f32),
+    near_spec = pl.BlockSpec((chips, LONG, WIDTH), lambda i, p: (near(i), 0, 0))
+    far_spec = pl.BlockSpec((chips, LONG, WIDTH), lambda i, p: (far(i), 0, 0))
+    sums = [
+        jax.ShapeDtypeStruct((WIDTH, GROUP), f32),
         jax.ShapeDtypeStruct((WIDTH, 2 * GROUP), f32),
         jax.ShapeDtypeStruct((8, WIDTH), f32),
         jax.ShapeDtypeStruct((8, GROUP), f32),
     ]
-    sum_specs = [whole(x.shape) for x in sum_shapes]
     return pl.pallas_call(
-        behind(functools.partial(long_backward_kernel, final), len(deps)),
+        behind(long_backward_kernel, len(deps)),
         grid_spec=pltpu.PrefetchScalarGridSpec(
             num_scalar_prefetch=1,
-            grid=(tiles,),
+            grid=(2 * tiles,),
             in_specs=[ANYWHERE] * len(deps)
             + [
                 pl.BlockSpec((BACK, STEPS * CHUNK), lambda i, p: (turn(i), 0)),
@@ -893,10 +889,10 @@
                 whole((STEPS * 8, CHUNK)),
                 once((WIDTH, 3 * WIDTH)),
                 whole(vectors.shape),
-            ]
-            + sum_specs[: len(sums)],
-            out_specs=[out_spec, out_spec, whole((WIDTH, GROUP))] + sum_specs,
+            ],
+            out_specs=[near_spec, near_spec, far_spec, far_spec] + [whole(x.shape) for x in sums],
             scratch_shapes=[
+                pltpu.VMEM((PARTS, GROUP, CHUNK), f32),
                 pltpu.VMEM((STEPS * CHUNK, GROUP), bf16),
                 pltpu.VMEM((STEPS * CHUNK, GROUP), bf16),
                 pltpu.VMEM((STEPS * 8, CHUNK), f32),
@@ -905,13 +901,13 @@
                 pltpu.VMEM((WIDTH, 2 * GROUP), bf16),
             ],
         ),
-        out_shape=[out, out, jax.ShapeDtypeStruct((WIDTH, GROUP), f32)] + sum_shapes,
+        out_shape=[out] * 4 + sums,
         compiler_params=pltpu.CompilerParams(**PARAMS),
         cost_estimate=pl.CostEstimate(
-            flops=20 * TILE * k.shape[0] * GROUP, bytes_accessed=16 << 20, transcendentals=0
+            flops=40 * TILE * k.shape[0] * GROUP, bytes_accessed=32 << 20, transcendentals=0
         ),
-        name="long_backward_final" if final else "long_backward",
-    )(place, *deps, e, k, vt, normed, q, mine, other, o, linv, weights, vectors, *sums)
+        name="long_backward",
+    )(place, *deps, e, k, vt, normed, q, mine, other, o, linv, weights, vectors)
 
 
 def short_backward_kernel(
@@ -1079,7 +1075,7 @@
     layout = Layout(lax.axis_size("band"), lax.axis_size("batch"))
     band = lax.axis_index("band")
     rows = incoming_rows[0]
-    ids = picture_label[0]
+    id_column = picture_label[0][:, None]
     upstream = loss_sensitivity[0]
     shard = layout.rows
     place = jnp.stack([band // 2, band % 2, band // 4, (band // 2) % 2, lax.axis_index("batch")]).astype(jnp.int32)
@@ -1095,7 +1091,9 @@
         second_offset,
     )
     if layout.pieces:
-        first_stack = layout.gather_depth(pack_first(triple_kernel, small, widening_offset))
+        first_stack = layout.gather_depth(
+            pack_first(triple_kernel, small, widening_offset), (place, id_column)
+        )
         first_plane = layout.gather_plane(first_stack)
         near = layout.gather_depth(pack_rows(rows, (first_stack,)), tuple(first_plane[1:]))
         first = layout.gather_core(first_plane)
@@ -1111,14 +1109,13 @@
         narrow = narrow.reshape(WIDTH // 16, 4, 16, WIDTH).transpose(0, 2, 1, 3).reshape(WIDTH, FF)
         second = [jnp.concatenate([second_stack, narrow], axis=1)]
     far = layout.flip(near, 2)
-
     n1, q_s, k_s, v_s, kt_s, vt_s, wqkv, vectors, hidden_shift = short_qkv(layout, place, rows, first)
     if layout.pieces:
         packed = pack_second(mixer_kernel, widening_kernel, narrowing_kernel, (n1,))
     else:
         hidden_shift = first[0][:, FIRST - 4 :].reshape(1, FF).astype(f32)
         packed = second[0]
-    e_s, o_s, linv_s, att_s = short_forward(q_s, k_s, vt_s, ids[LONG:], (near, packed))
+    e_s, o_s, linv_s, att_s = short_forward(q_s, k_s, vt_s, id_column, picture_label, (near, packed))
     if layout.pieces:
         second_stack = layout.gather_depth(packed, (linv_s,))
         second_plane = layout.gather_plane(second_stack)
@@ -1130,29 +1127,28 @@
     if layout.pieces:
         second = layout.gather_core(second_plane[:1] + list(tie(second_plane[1:], (att_keep,))))
     layer_out, mid_l, mid_s, da_keep, da_send, da_s, feed_rows, hidden_sum, *second_grads = feed(
-        layout, place, rows, ids, upstream, att_keep, layout.flip(att_send, 1), att_s, vectors, hidden_shift, second
+        layout, place, rows, id_column, upstream, att_keep, layout.flip(att_send, 1), att_s, vectors, hidden_shift, second
     )
     da_other = layout.flip(da_send, 1)
     inputs = (place, e_l, k_l, vt_l, n1_l, q_l, da_keep, da_other, o_l, linv_l, wqkv, vectors)
 
     pairs = layout.scatter_core(second_grads) if layout.pieces else []
-    keep_x, send_x, _, *sums = long_backward(layout, False, *inputs, (), tuple(pairs[1:]))
-    moved = (keep_x.astype(f32) + layout.flip(send_x, 1).astype(f32)).astype(bf16)
+    keep0, send0, keep1, send1, gq, gkv, long_sums, long_side = long_backward(layout, *inputs, tuple(pairs[1:]))
+    moved = (keep1.astype(f32) + layout.flip(send1, 1).astype(f32)).astype(bf16)
     totals = layout.scatter_plane(pairs) if layout.pieces else []
-    keep, send, gq, _, gkv, long_sums, long_side = long_backward(
-        layout, True, *inputs, sums, (moved, *totals[1:])
-    )
-    dx_totals = layout.add_depth([keep, layout.flip(send, 1), layout.flip(moved, 2)])
     dx_s, *first_grads = short_backward(
         layout, place, e_s, k_s, v_s, q_s, kt_s, da_s, o_s, linv_s, n1, rows, mid_s, wqkv, vectors,
-        gq, gkv, long_sums, long_side, feed_rows, hidden_sum, tuple(dx_totals[1:]),
+        gq, gkv, long_sums, long_side, feed_rows, hidden_sum, (moved, *totals[1:]),
     )
+    dx_totals = layout.add_depth([keep0, layout.flip(send0, 1), layout.flip(moved, 2)])
     dx_long = layout.scatter_depth(dx_totals, -1)
     if layout.pieces:
         second_grad = layout.scatter_depth(totals)
         narrow_grad = second_grad[:, WIDTH + FF :].reshape(shard, 4, WIDTH).transpose(1, 0, 2)
         narrow_grad = narrow_grad.reshape(4 * shard, WIDTH)
-        first_grad = layout.scatter_depth(layout.scatter_plane(layout.scatter_core(first_grads)))
+        first_grad = layout.scatter_depth(
+            layout.scatter_plane(layout.scatter_core(first_grads, tuple(dx_totals[1:])))
+        )
         hidden_grad = first_grad[0, FIRST - 4 * shard :]
     else:
         packed = second_grads[0][:, WIDTH + FF :].reshape(WIDTH // 16, 16, 4, WIDTH).transpose(0, 2, 1, 3)

time: 268 us -> 266 us (level)
  Pallas kernels: 140 us -> 136 us
  other arithmetic: 11 us -> 14.1 us
    ppermute x12, waiting for transfers between devices: 24.9 us -> 11.9 us  [shift_plane(): return lax.ppermute(block, ('band', 'batch'), pairs)]
    ppermute x18, waiting for transfers between devices: 11.1 us -> 21 us  [shift_depth(): return lax.ppermute(block, 'band', pairs)]
    pallas_call x2 -> x1, Pallas kernels: 36.9 us -> 32.5 us  [long_backward(): pl.pallas_call(behind(long_backward_kernel, len(deps)), grid_spec=pltpu.P...]
    unnamed x88 -> x96, local copies, waits for them, and re-layouts: 10.2 us -> 11.1 us
  transfers between devices with their start and end apart: 48 -> 48, of which waited for: 16 -> 15; matrix products, arithmetic and copies ran while one was open for 5% -> 6% of each run, Pallas kernels for 41% -> 40%
where the time goes in v1:
time: 266 us; the launch traced here: 262 us
  Pallas kernels  136 us (51%)
  starting transfers between devices  51.6 us (19%)
  waiting for transfers between devices  40.7 us (15%)
  local copies, waits for them, and re-layouts  18.3 us (7%)
  other arithmetic  14.1 us (5%)
    pallas_call x1, Pallas kernels, long_backward(): pl.pallas_call(behind(long_backward_kernel, len(deps)), grid_spec=pltpu.P...  32.5 us
    ppermute x18, starting transfers between devices, shift_depth(): return lax.ppermute(block, 'band', pairs)  31.9 us
    pallas_call x1, Pallas kernels, feed(): pl.pallas_call(functools.partial(feed_kernel, layout), grid_spec=pltpu.Pr...  25.4 us
    pallas_call x1, Pallas kernels, short_backward(): pl.pallas_call(behind(functools.partial(short_backward_kernel, layout), l...  22.3 us
    ppermute x18, waiting for transfers between devices, shift_depth(): return lax.ppermute(block, 'band', pairs)  21 us
    pallas_call x1, Pallas kernels, long_forward(): pl.pallas_call(long_forward_kernel, grid=(STEPS + 1,), in_specs=[once((TI...  15 us
    ppermute x12, starting transfers between devices, shift_plane(): return lax.ppermute(block, ('band', 'batch'), pairs)  14.3 us
    pallas_call x1, Pallas kernels, short_forward(): pl.pallas_call(behind(short_forward_kernel, len(deps), False), grid=(HEAD...  12.5 us
  transfers between devices with their start and end apart: 48, of which 15 were waited for; matrix products, arithmetic and copies ran while one was open for 6% of the time, Pallas kernels for 40%

profile of v1, /device:TPU:0, one launch (start us, length us, event | category | flops | bytes accessed | tf_op | source)
XLA Modules:
  0.0 262.1 jit_solution(8763586471028168906)
XLA Ops:
  0.7 1.7 pack_first.1.refs_2_
  2.3 3.0 %collective-permute-start = (bf16[16,1664]{1,0:T(8,128)(2,1)}, bf16[16,1664]{1,0:T(8,128)(2,1)S(1)}, u32[]{:S(2)}, u32[]{:S(2)}) collective-permute-start(bf16[16,1664]{1,0:T(8,128)(2,1)} %pack_first.1.refs_2_), channel_id=1, source_target_pairs={{0,8},{2,10},{4,12},{6,14},{8,16},{10,18},{12,20},{14,22},{16,24},... | collective-permute-start | bytes 159752 | tf_op jit(solution)/shard_map/ppermute | solution.py:102
  5.3 2.6 collective-permute-start.1
  7.9 1.3 collective-permute-start.2
  9.3 1.7 copy.39.refs_1_.refs_5_.ids_ref
  13.2 1.6 stack_blocks.3.refs_0_
  14.8 1.9 collective-permute-start.3
  16.7 1.7 pack_rows.1.refs_3_
  18.9 2.6 collective-permute-start.7
  21.4 1.0 collective-permute-start.8
  22.5 1.5 collective-permute-start.4
  24.4 5.0 %collective-permute-done.4.refs_1_.refs_2_ = bf16[4,16,1664]{2,1,0:T(8,128)(2,1)S(1)} collective-permute-done((bf16[4,16,1664]{2,1,0:T(8,128)(2,1)}, bf16[4,16,1664]{2,1,0:T(8,128)(2,1)S(1)}, u32[]{:S(2)}, u32[]{:S(2)}) %collective-permute-start.4) | collective-permute-done | bytes 213024 | tf_op jit(solution)/shard_map/ppermute | solution.py:112
  29.3 2.8 %collective-permute-done.5.refs_2_.refs_3_ = bf16[4,16,1664]{2,1,0:T(8,128)(2,1)S(1)} collective-permute-done((bf16[4,16,1664]{2,1,0:T(8,128)(2,1)}, bf16[4,16,1664]{2,1,0:T(8,128)(2,1)S(1)}, u32[]{:S(2)}, u32[]{:S(2)}) %collective-permute-start.5) | collective-permute-done | bytes 213024 | tf_op jit(solution)/shard_map/ppermute | solution.py:112
  32.1 5.9 %collective-permute-done.7.refs_5_ = bf16[256,512]{1,0:T(8,128)(2,1)S(1)} collective-permute-done((bf16[256,512]{1,0:T(8,128)(2,1)}, bf16[256,512]{1,0:T(8,128)(2,1)S(1)}, u32[]{:S(2)}, u32[]{:S(2)}) %collective-permute-start.7) | collective-permute-done | bytes 262176 | tf_op jit(solution)/shard_map/ppermute | solution.py:102
  38.7 0.7 copy-done.24
  39.4 2.2 stack_blocks.4.refs_0_.refs_2_
  41.6 1.5 collective-permute-start.17
  44.1 0.7 collective-permute-done.9.refs_4_
  46.1 0.7 copy-done.45
  46.8 6.9 %short_qkv.1 = (bf16[768,512]{1,0:T(8,128)(2,1)}, bf16[768,512]{1,0:T(8,128)(2,1)}, bf16[768,512]{1,0:T(8,128)(2,1)}, bf16[768,512]{1,0:T(8,128)(2,1)}, bf16[512...) custom-call(s32[5]{0:T(128)} %stack.23.refs_0_.place_ref, ...), custom_call_target="tpu_custom_call" | custom-call | flops 1207959552 | bytes 10485760 | tf_op jit(solution)/shard_map/short_qkv/pallas_call | solution.py:317
  53.7 1.7 pack_second.1.refs_1_
  55.3 5.4 %collective-permute-start.13 = (bf16[16,4608]{1,0:T(8,128)(2,1)}, bf16[16,4608]{1,0:T(8,128)(2,1)S(1)}, u32[]{:S(2)}, u32[]{:S(2)}) collective-permute-start(bf16[16,4608]{1,0:T(8,128)(2,1)} %pack_second.1.refs_1_), channel_id=1, source_target_pairs={{0,8},{2,10},{4,12},{6,14},{8,16},{10,18},{12,20},{14,22},{16,24},... | collective-permute-start | bytes 442376 | tf_op jit(solution)/shard_map/ppermute | solution.py:102
  60.7 0.8 collective-permute-start.14
  61.6 2.0 collective-permute-start.15
  63.6 12.5 %short_forward.1 = (bf16[768,6144]{1,0:T(8,128)(2,1)}, f32[512,768]{1,0:T(8,128)}, f32[64,768]{1,0:T(8,128)}, bf16[768,512]{1,0:T(8,128)(2,1)}) custom-call(bf16[4,256,512]{2,1,0:T(8,128)(2,1)} %stack_blocks.4.refs_0_.refs_2_, bf16[16,4608]{1,0:T(8,128)(2,1)} %pack_second.1.refs_1_, bf16[768,512]{1,0:T(8,128)(2,1)} %get-tuple-element.62.refs_2_.refs_8_, ...), custom_call_target="tpu_custom_call" | custom-call | flops 3623878656 | bytes 12582912 | tf_op jit(solution)/shard_map/short_forward/pallas_call | solution.py:402
  76.8 2.0 stack_blocks.5.refs_1_.refs_0_
  78.8 1.0 copy-done.10
  80.8 0.9 collective-permute-start.21
  81.6 2.1 collective-permute-start.22
  83.8 0.9 copy-done.37
  85.1 10.6 %long_prepare.1 = (bf16[4096,512]{1,0:T(8,128)(2,1)}, bf16[512,256]{1,0:T(8,128)(2,1)}, bf16[4096,256]{1,0:T(8,128)(2,1)}, bf16[256,4096]{1,0:T(8,128)(2,1)}) custom-call(s32[5]{0:T(128)} %stack.23.refs_0_.place_ref, bf16[4,16,4608]{2,1,0:T(8,128)(2,1)} %stack_blocks.5.refs_1_.refs_0_, bf16[4,256,512]{2,1,0:T(8,128)(2,1)} %stack_blocks.4.refs_0_.refs_2_, ...), custom_call_target="tpu_custom_call" | custom-call | flops 2147483648 | bytes 18874368 | tf_op jit(solution)/shard_map/long_prepare/pallas_call | solution.py:488
  95.6 15.0 %long_forward.1 = (bf16[4096,2048]{1,0:T(8,128)(2,1)}, f32[2,256,256]{2,1,0:T(8,128)}, f32[64,256]{1,0:T(8,128)}, bf16[256,256]{1,0:T(8,128)(2,1)}, bf16[256,256]{1,0:T(8,128)(2,1)}) custom-call(bf16[512,256]{1,0:T(8,128)(2,1)} %get-tuple-element.68.q_ref.refs_8_, bf16[4096,256]{1,0:T(8,128)(2,1)} %get-tuple-element.69.k_ref.refs_5_, ...), custom_call_target="tpu_custom_call" | custom-call | flops 8589934592 | bytes 25165824 | tf_op jit(solution)/shard_map/long_forward/pallas_call | solution.py:608
  110.7 0.8 copy-done.16
  112.9 3.1 %collective-permute-done.19.other_ref = bf16[256,256]{1,0:T(8,128)(2,1)S(1)} collective-permute-done((bf16[256,256]{1,0:T(8,128)(2,1)}, bf16[256,256]{1,0:T(8,128)(2,1)S(1)}, u32[]{:S(2)}, u32[]{:S(2)}) %collective-permute-start.19) | collective-permute-done | bytes 131104 | tf_op jit(solution)/shard_map/ppermute | solution.py:105
  117.2 25.4 %feed.1 = (bf16[1024,512]{1,0:T(8,128)(2,1)}, f32[256,512]{1,0:T(8,128)}, f32[768,512]{1,0:T(8,128)}, bf16[256,256]{1,0:T(8,128)(2,1)}, bf16[256,256]{1,0:T(8,12...) custom-call(s32[5]{0:T(128)} %stack.23.refs_0_.place_ref, ...), custom_call_target="tpu_custom_call" | custom-call | flops 14495514624 | bytes 18874368 | tf_op jit(solution)/shard_map/feed/pallas_call | solution.py:736
  143.1 0.7 slice.262
  144.2 3.2 %collective-permute-done.27 = bf16[4,4,16,4608]{3,2,1,0:T(8,128)(2,1)S(1)} collective-permute-done((bf16[4,4,16,4608]{3,2,1,0:T(8,128)(2,1)}, bf16[4,4,16,4608]{3,2,1,0:T(8,128)(2,1)S(1)}, u32[]{:S(2)}, u32[]{:S(2)}) %collective-permute-start.27) | collective-permute-done | bytes 2359328 | tf_op jit(solution)/shard_map/ppermute | solution.py:105
  147.4 2.3 add_convert_fusion.1
  150.3 0.9 collective-permute-start.36
  151.1 2.1 collective-permute-start.37
  153.9 32.5 %long_backward.1 = (bf16[4,256,512]{2,1,0:T(8,128)(2,1)}, bf16[4,256,512]{2,1,0:T(8,128)(2,1)}, bf16[4,256,512]{2,1,0:T(8,128)(2,1)}, bf16[4,256,512]{2,1,0:T(8,...) custom-call(s32[5]{0:T(128)} %stack.23.refs_0_.place_ref, ...), custom_call_target="tpu_custom_call" | custom-call | flops 21474836480 | bytes 33554432 | tf_op jit(solution)/shard_map/long_backward/pallas_call | solution.py:874
  187.8 2.1 collective-permute-start.46
  190.0 1.2 collective-permute-start.47
  192.6 22.3 %short_backward.1 = (bf16[768,512]{1,0:T(8,128)(2,1)}, bf16[4,4,16,1664]{3,2,1,0:T(8,128)(2,1)}, bf16[4,4,16,1664]{3,2,1,0:T(8,128)(2,1)}) custom-call(s32[5]{0:T(128)} %stack.23.refs_0_.place_ref, bf16[4,256,512]{2,1,0:T(8,128)(2,1)} %copy-done.5, bf16[16,4608]{1,0:T(8,128)(2,1)} %copy-done.30, bf16[16,4608]{1,0:T(8,128)(2,1)} %copy-done.29, ...), custom_call_target="tpu_custom_call" | custom-call | flops 7247757312 | bytes 18874368 | tf_op jit(solution)/shard_map/short_backward/pallas_call | solution.py:1008
  215.0 1.1 fusion.22
  216.3 2.5 fusion.32
  218.8 0.9 copy-done.2
  219.7 2.6 add_convert_fusion.11
  222.8 0.9 collective-permute-start.40
  223.7 2.1 collective-permute-start.41
  225.8 0.7 fusion.61
  227.2 0.7 copy.40
  227.9 1.5 collective-permute-start.32
  230.1 1.7 collective-permute-start.34
  231.8 4.1 %collective-permute-done.41 = bf16[4,16,1664]{2,1,0:T(8,128)(2,1)} collective-permute-done((bf16[4,16,1664]{2,1,0:T(8,128)(2,1)}, bf16[4,16,1664]{2,1,0:T(8,128)(2,1)}, u32[]{:S(2)}, u32[]{:S(2)}) %collective-permute-start.41) | collective-permute-done | bytes 213024 | tf_op jit(solution)/shard_map/ppermute | solution.py:112
  235.8 1.1 fusion.56
  237.0 0.8 collective-permute-start.42
  237.8 1.3 collective-permute-start.43
  239.1 2.8 %collective-permute-start.44 = (bf16[16,1664]{1,0:T(8,128)(2,1)S(1)}, bf16[16,1664]{1,0:T(8,128)(2,1)S(1)}, u32[]{:S(2)}, u32[]{:S(2)}) collective-permute-start(bf16[16,1664]{1,0:T(8,128)(2,1)S(1)} %get-tuple-element.133), channel_id=1, source_target_pairs={{0,24},{2,26},{4,28},{6,30},{8,0},{10,2},{12,4},{14,6},{16,8},{18,... | collective-permute-start | bytes 159752 | tf_op jit(solution)/shard_map/ppermute | solution.py:102
  242.0 14.2 %collective-permute-done.33 = bf16[256,512]{1,0:T(8,128)(2,1)S(1)} collective-permute-done((bf16[256,512]{1,0:T(8,128)(2,1)S(1)}, bf16[256,512]{1,0:T(8,128)(2,1)S(1)}, u32[]{:S(2)}, u32[]{:S(2)}) %collective-permute-start.33) | collective-permute-done | bytes 262176 | tf_op jit(solution)/shard_map/ppermute | solution.py:102
  256.2 1.4 fusion.59
  257.9 1.0 maximum_bitcast_fusion
  258.9 0.9 fusion.55
  260.5 0.8 slice_reduce_fusion
  (170 shorter events, 19.1 us)
Async XLA Ops:
  2.3 9.3 %collective-permute-start = (bf16[16,1664]{1,0:T(8,128)(2,1)}, bf16[16,1664]{1,0:T(8,128)(2,1)S(1)}, u32[]{:S(2)}, u32[]{:S(2)}) collective-permute-start(bf16[16,1664]{1,0:T(8,128)(2,1)} %pack_first.1.refs_2_), channel_id=1, source_target_pairs={{0,8},{2,10},{4,12},{6,14},{8,16},{10,18},{12,20},{14,22},{16,24},... | collective-permute-start | bytes 159752 | tf_op jit(solution)/shard_map/ppermute | solution.py:102
  5.3 6.6 %collective-permute-start.1 = (bf16[16,1664]{1,0:T(8,128)(2,1)}, bf16[16,1664]{1,0:T(8,128)(2,1)S(1)}, u32[]{:S(2)}, u32[]{:S(2)}) collective-permute-start(bf16[16,1664]{1,0:T(8,128)(2,1)} %pack_first.1.refs_2_), channel_id=1, source_target_pairs={{0,16},{2,18},{4,20},{6,22},{8,24},{10,26},{12,28},{14,30},{16,0},... | collective-permute-start | bytes 159752 | tf_op jit(solution)/shard_map/ppermute | solution.py:102
  7.9 4.5 %collective-permute-start.2 = (bf16[16,1664]{1,0:T(8,128)(2,1)}, bf16[16,1664]{1,0:T(8,128)(2,1)S(1)}, u32[]{:S(2)}, u32[]{:S(2)}) collective-permute-start(bf16[16,1664]{1,0:T(8,128)(2,1)} %pack_first.1.refs_2_), channel_id=1, source_target_pairs={{0,24},{2,26},{4,28},{6,30},{8,0},{10,2},{12,4},{14,6},{16,8},{18,... | collective-permute-start | bytes 159752 | tf_op jit(solution)/shard_map/ppermute | solution.py:102
  14.8 9.2 %collective-permute-start.3 = (bf16[4,16,1664]{2,1,0:T(8,128)(2,1)}, bf16[4,16,1664]{2,1,0:T(8,128)(2,1)S(1)}, u32[]{:S(2)}, u32[]{:S(2)}) collective-permute-start(bf16[4,16,1664]{2,1,0:T(8,128)(2,1)} %stack_blocks.3.refs_0_), channel_id=1, source_target_pairs={{0,1},{1,0},{2,3},{3,2},{4,5},{5,4},{6,7},{7,6},{8,9},{9,8},{10,11... | collective-permute-start | bytes 638984 | tf_op jit(solution)/shard_map/ppermute | solution.py:112
  16.7 26.4 %copy-start.11 = (bf16[4,16,1664]{2,1,0:T(8,128)(2,1)S(1)}, bf16[4,16,1664]{2,1,0:T(8,128)(2,1)}, u32[]{:S(2)}) copy-start(bf16[4,16,1664]{2,1,0:T(8,128)(2,1)} %stack_blocks.3.refs_0_) | copy-start | bytes 638980
  18.4 13.7 %collective-permute-start.6 = (bf16[256,512]{1,0:T(8,128)(2,1)}, bf16[256,512]{1,0:T(8,128)(2,1)S(1)}, u32[]{:S(2)}, u32[]{:S(2)}) collective-permute-start(bf16[256,512]{1,0:T(8,128)(2,1)} %pack_rows.1.refs_3_), channel_id=1, source_target_pairs={{0,8},{2,10},{4,12},{6,14},{8,16},{10,18},{12,20},{14,22},{16,24},... | collective-permute-start | bytes 786440 | tf_op jit(solution)/shard_map/ppermute | solution.py:102
  18.9 19.1 %collective-permute-start.7 = (bf16[256,512]{1,0:T(8,128)(2,1)}, bf16[256,512]{1,0:T(8,128)(2,1)S(1)}, u32[]{:S(2)}, u32[]{:S(2)}) collective-permute-start(bf16[256,512]{1,0:T(8,128)(2,1)} %pack_rows.1.refs_3_), channel_id=1, source_target_pairs={{0,16},{2,18},{4,20},{6,22},{8,24},{10,26},{12,28},{14,30},{16,0},... | collective-permute-start | bytes 786440 | tf_op jit(solution)/shard_map/ppermute | solution.py:102
  21.4 16.6 %collective-permute-start.8 = (bf16[256,512]{1,0:T(8,128)(2,1)}, bf16[256,512]{1,0:T(8,128)(2,1)S(1)}, u32[]{:S(2)}, u32[]{:S(2)}) collective-permute-start(bf16[256,512]{1,0:T(8,128)(2,1)} %pack_rows.1.refs_3_), channel_id=1, source_target_pairs={{0,24},{2,26},{4,28},{6,30},{8,0},{10,2},{12,4},{14,6},{16,8},{18,... | collective-permute-start | bytes 786440 | tf_op jit(solution)/shard_map/ppermute | solution.py:102
  22.5 6.9 %collective-permute-start.4 = (bf16[4,16,1664]{2,1,0:T(8,128)(2,1)}, bf16[4,16,1664]{2,1,0:T(8,128)(2,1)S(1)}, u32[]{:S(2)}, u32[]{:S(2)}) collective-permute-start(bf16[4,16,1664]{2,1,0:T(8,128)(2,1)} %stack_blocks.3.refs_0_), channel_id=1, source_target_pairs={{0,4},{1,5},{2,6},{3,7},{4,0},{5,1},{6,2},{7,3},{8,12},{9,13},{10,... | collective-permute-start | bytes 638984 | tf_op jit(solution)/shard_map/ppermute | solution.py:112
  24.0 14.0 %copy-start.25 = (bf16[4,16,1664]{2,1,0:T(8,128)(2,1)}, bf16[4,16,1664]{2,1,0:T(8,128)(2,1)S(1)}, u32[]{:S(2)}) copy-start(bf16[4,16,1664]{2,1,0:T(8,128)(2,1)S(1)} %collective-permute-done.3.refs_0_.refs_1_) | copy-start | bytes 638980
  24.0 8.1 %collective-permute-start.5 = (bf16[4,16,1664]{2,1,0:T(8,128)(2,1)}, bf16[4,16,1664]{2,1,0:T(8,128)(2,1)S(1)}, u32[]{:S(2)}, u32[]{:S(2)}) collective-permute-start(bf16[4,16,1664]{2,1,0:T(8,128)(2,1)} %stack_blocks.3.refs_0_), channel_id=1, source_target_pairs={{0,5},{1,4},{2,7},{3,6},{4,1},{5,0},{6,3},{7,2},{8,13},{9,12},{10,... | collective-permute-start | bytes 638984 | tf_op jit(solution)/shard_map/ppermute | solution.py:112
  29.3 8.7 %copy-start.26 = (bf16[4,16,1664]{2,1,0:T(8,128)(2,1)}, bf16[4,16,1664]{2,1,0:T(8,128)(2,1)S(1)}, u32[]{:S(2)}) copy-start(bf16[4,16,1664]{2,1,0:T(8,128)(2,1)S(1)} %collective-permute-done.4.refs_1_.refs_2_) | copy-start | bytes 638980
  32.1 5.9 %copy-start.27 = (bf16[4,16,1664]{2,1,0:T(8,128)(2,1)}, bf16[4,16,1664]{2,1,0:T(8,128)(2,1)S(1)}, u32[]{:S(2)}) copy-start(bf16[4,16,1664]{2,1,0:T(8,128)(2,1)S(1)} %collective-permute-done.5.refs_2_.refs_3_) | copy-start | bytes 638980
  32.1 5.9 %copy-start.22 = (bf16[256,512]{1,0:T(8,128)(2,1)}, bf16[256,512]{1,0:T(8,128)(2,1)S(1)}, u32[]{:S(2)}) copy-start(bf16[256,512]{1,0:T(8,128)(2,1)S(1)} %collective-permute-done.6.refs_4_) | copy-start | bytes 786436
  41.6 37.2 %collective-permute-start.17 = (bf16[4,256,512]{2,1,0:T(8,128)(2,1)}, bf16[4,256,512]{2,1,0:T(8,128)(2,1)S(1)}, u32[]{:S(2)}, u32[]{:S(2)}) collective-permute-start(bf16[4,256,512]{2,1,0:T(8,128)(2,1)} %stack_blocks.4.refs_0_.refs_2_), channel_id=1, source_target_pairs={{0,4},{2,6},{4,0},{6,2},{8,12},{10,14},{12,8},{14,10},{16,20},{18,... | collective-permute-start | bytes 3145736 | tf_op jit(solution)/shard_map/ppermute | solution.py:105
  43.1 1.7 collective-permute-start.9
  43.1 2.0 collective-permute-start.10
  43.6 1.8 collective-permute-start.11
  43.6 2.1 collective-permute-start.12
  44.9 38.9 %collective-permute-start.16 = (bf16[4,256,512]{2,1,0:T(8,128)(2,1)}, bf16[4,256,512]{2,1,0:T(8,128)(2,1)S(1)}, u32[]{:S(2)}, u32[]{:S(2)}) collective-permute-start(bf16[4,256,512]{2,1,0:T(8,128)(2,1)} %stack_blocks.4.refs_0_.refs_2_), channel_id=1, source_target_pairs={{0,2},{2,0},{4,6},{6,4},{8,10},{10,8},{12,14},{14,12},{16,18},{18,... | collective-permute-start | bytes 3145736 | tf_op jit(solution)/shard_map/ppermute | solution.py:105
  55.3 20.7 %collective-permute-start.13 = (bf16[16,4608]{1,0:T(8,128)(2,1)}, bf16[16,4608]{1,0:T(8,128)(2,1)S(1)}, u32[]{:S(2)}, u32[]{:S(2)}) collective-permute-start(bf16[16,4608]{1,0:T(8,128)(2,1)} %pack_second.1.refs_1_), channel_id=1, source_target_pairs={{0,8},{2,10},{4,12},{6,14},{8,16},{10,18},{12,20},{14,22},{16,24},... | collective-permute-start | bytes 442376 | tf_op jit(solution)/shard_map/ppermute | solution.py:102
  60.7 15.3 %collective-permute-start.14 = (bf16[16,4608]{1,0:T(8,128)(2,1)}, bf16[16,4608]{1,0:T(8,128)(2,1)S(1)}, u32[]{:S(2)}, u32[]{:S(2)}) collective-permute-start(bf16[16,4608]{1,0:T(8,128)(2,1)} %pack_second.1.refs_1_), channel_id=1, source_target_pairs={{0,16},{2,18},{4,20},{6,22},{8,24},{10,26},{12,28},{14,30},{16,0},... | collective-permute-start | bytes 442376 | tf_op jit(solution)/shard_map/ppermute | solution.py:102
  61.6 14.5 %collective-permute-start.15 = (bf16[16,4608]{1,0:T(8,128)(2,1)}, bf16[16,4608]{1,0:T(8,128)(2,1)S(1)}, u32[]{:S(2)}, u32[]{:S(2)}) collective-permute-start(bf16[16,4608]{1,0:T(8,128)(2,1)} %pack_second.1.refs_1_), channel_id=1, source_target_pairs={{0,24},{2,26},{4,28},{6,30},{8,0},{10,2},{12,4},{14,6},{16,8},{18,... | collective-permute-start | bytes 442376 | tf_op jit(solution)/shard_map/ppermute | solution.py:102
  79.8 4.0 %collective-permute-start.18 = (bf16[4,256,512]{2,1,0:T(8,128)(2,1)}, bf16[4,256,512]{2,1,0:T(8,128)(2,1)S(1)}, u32[]{:S(2)}, u32[]{:S(2)}) collective-permute-start(bf16[4,256,512]{2,1,0:T(8,128)(2,1)} %tie.3.refs_4_), channel_id=1, source_target_pairs={{0,2},{2,0},{4,6},{6,4},{8,10},{10,8},{12,14},{14,12},{16,18},{18,... | collective-permute-start | bytes 3145736 | tf_op jit(solution)/shard_map/ppermute | solution.py:105
  80.3 30.4 %collective-permute-start.20 = (bf16[4,16,4608]{2,1,0:T(8,128)(2,1)S(1)}, bf16[4,16,4608]{2,1,0:T(8,128)(2,1)S(1)}, u32[]{:S(2)}, u32[]{:S(2)}) collective-permute-start(bf16[4,16,4608]{2,1,0:T(8,128)(2,1)S(1)} %copy-done.3), channel_id=1, source_target_pairs={{0,1},{1,0},{2,3},{3,2},{4,5},{5,4},{6,7},{7,6},{8,9},{9,8},{10,11... | collective-permute-start | bytes 1769480 | tf_op jit(solution)/shard_map/ppermute | solution.py:112
  80.8 29.9 %collective-permute-start.21 = (bf16[4,16,4608]{2,1,0:T(8,128)(2,1)S(1)}, bf16[4,16,4608]{2,1,0:T(8,128)(2,1)S(1)}, u32[]{:S(2)}, u32[]{:S(2)}) collective-permute-start(bf16[4,16,4608]{2,1,0:T(8,128)(2,1)S(1)} %copy-done.3), channel_id=1, source_target_pairs={{0,4},{1,5},{2,6},{3,7},{4,0},{5,1},{6,2},{7,3},{8,12},{9,13},{10,... | collective-permute-start | bytes 1769480 | tf_op jit(solution)/shard_map/ppermute | solution.py:112
  81.6 29.1 %collective-permute-start.22 = (bf16[4,16,4608]{2,1,0:T(8,128)(2,1)S(1)}, bf16[4,16,4608]{2,1,0:T(8,128)(2,1)S(1)}, u32[]{:S(2)}, u32[]{:S(2)}) collective-permute-start(bf16[4,16,4608]{2,1,0:T(8,128)(2,1)S(1)} %copy-done.3), channel_id=1, source_target_pairs={{0,5},{1,4},{2,7},{3,6},{4,1},{5,0},{6,3},{7,2},{8,13},{9,12},{10,... | collective-permute-start | bytes 1769480 | tf_op jit(solution)/shard_map/ppermute | solution.py:112
  83.8 29.1 %collective-permute-start.23 = (bf16[4,16,4608]{2,1,0:T(8,128)(2,1)S(1)}, bf16[4,16,4608]{2,1,0:T(8,128)(2,1)}, u32[]{:S(2)}, u32[]{:S(2)}) collective-permute-start(bf16[4,16,4608]{2,1,0:T(8,128)(2,1)S(1)} %copy-done.3), channel_id=1, source_target_pairs={{0,2},{2,0},{4,6},{6,4},{8,10},{10,8},{12,14},{14,12},{16,18},{18,... | collective-permute-start | bytes 1769480 | tf_op jit(solution)/shard_map/ppermute | solution.py:105
  111.9 4.1 %collective-permute-start.24 = (bf16[4,16,4608]{2,1,0:T(8,128)(2,1)}, bf16[4,16,4608]{2,1,0:T(8,128)(2,1)S(1)}, u32[]{:S(2)}, u32[]{:S(2)}) collective-permute-start(bf16[4,16,4608]{2,1,0:T(8,128)(2,1)} %get-tuple-element.75.refs_1_), channel_id=1, source_target_pairs={{0,2},{2,0},{4,6},{6,4},{8,10},{10,8},{12,14},{14,12},{16,18},{18,... | collective-permute-start | bytes 1769480 | tf_op jit(solution)/shard_map/ppermute | solution.py:105
  112.1 3.9 %collective-permute-start.25 = (bf16[4,16,4608]{2,1,0:T(8,128)(2,1)}, bf16[4,16,4608]{2,1,0:T(8,128)(2,1)S(1)}, u32[]{:S(2)}, u32[]{:S(2)}) collective-permute-start(bf16[4,16,4608]{2,1,0:T(8,128)(2,1)} %get-tuple-element.76.refs_2_), channel_id=1, source_target_pairs={{0,2},{2,0},{4,6},{6,4},{8,10},{10,8},{12,14},{14,12},{16,18},{18,... | collective-permute-start | bytes 1769480 | tf_op jit(solution)/shard_map/ppermute | solution.py:105
  112.4 3.6 %collective-permute-start.26 = (bf16[4,16,4608]{2,1,0:T(8,128)(2,1)}, bf16[4,16,4608]{2,1,0:T(8,128)(2,1)S(1)}, u32[]{:S(2)}, u32[]{:S(2)}) collective-permute-start(bf16[4,16,4608]{2,1,0:T(8,128)(2,1)} %get-tuple-element.77.refs_3_), channel_id=1, source_target_pairs={{0,2},{2,0},{4,6},{6,4},{8,10},{10,8},{12,14},{14,12},{16,18},{18,... | collective-permute-start | bytes 1769480 | tf_op jit(solution)/shard_map/ppermute | solution.py:105
  112.6 3.4 %collective-permute-start.19 = (bf16[256,256]{1,0:T(8,128)(2,1)}, bf16[256,256]{1,0:T(8,128)(2,1)S(1)}, u32[]{:S(2)}, u32[]{:S(2)}) collective-permute-start(bf16[256,256]{1,0:T(8,128)(2,1)} %get-tuple-element.72), channel_id=1, source_target_pairs={{0,2},{2,0},{4,6},{6,4},{8,10},{10,8},{12,14},{14,12},{16,18},{18,... | collective-permute-start | bytes 393224 | tf_op jit(solution)/shard_map/ppermute | solution.py:105
  117.2 25.6 %copy-start = (bf16[1,1024,512]{2,1,0:T(8,128)(2,1)S(1)}, bf16[1,1024,512]{2,1,0:T(8,128)(2,1)}, u32[]{:S(2)}) copy-start(bf16[1,1024,512]{2,1,0:T(8,128)(2,1)} %param.16) | copy-start | bytes 3145732
  142.6 4.7 %collective-permute-start.27 = (bf16[4,4,16,4608]{3,2,1,0:T(8,128)(2,1)}, bf16[4,4,16,4608]{3,2,1,0:T(8,128)(2,1)S(1)}, u32[]{:S(2)}, u32[]{:S(2)}) collective-permute-start(bf16[4,4,16,4608]{3,2,1,0:T(8,128)(2,1)} %get-tuple-element.81), channel_id=1, source_target_pairs={{0,2},{2,0},{4,6},{6,4},{8,10},{10,8},{12,14},{14,12},{16,18},{18,... | collective-permute-start | bytes 7077896 | tf_op jit(solution)/shard_map/ppermute | solution.py:105
  143.9 9.4 %collective-permute-start.28 = (bf16[256,256]{1,0:T(8,128)(2,1)}, bf16[256,256]{1,0:T(8,128)(2,1)S(1)}, u32[]{:S(2)}, u32[]{:S(2)}) collective-permute-start(bf16[256,256]{1,0:T(8,128)(2,1)} %get-tuple-element.85), channel_id=1, source_target_pairs={{0,2},{2,0},{4,6},{6,4},{8,10},{10,8},{12,14},{14,12},{16,18},{18,... | collective-permute-start | bytes 393224 | tf_op jit(solution)/shard_map/ppermute | solution.py:105
  149.7 37.3 %collective-permute-start.35 = (bf16[4,16,4608]{2,1,0:T(8,128)(2,1)S(1)}, bf16[4,16,4608]{2,1,0:T(8,128)(2,1)S(1)}, u32[]{:S(2)}, u32[]{:S(2)}) collective-permute-start(bf16[4,16,4608]{2,1,0:T(8,128)(2,1)S(1)} %get-tuple-element.121.refs_1_), channel_id=1, source_target_pairs={{0,1},{1,0},{2,3},{3,2},{4,5},{5,4},{6,7},{7,6},{8,9},{9,8},{10,11... | collective-permute-start | bytes 1769480 | tf_op jit(solution)/shard_map/ppermute | solution.py:112
  150.3 36.8 %collective-permute-start.36 = (bf16[4,16,4608]{2,1,0:T(8,128)(2,1)S(1)}, bf16[4,16,4608]{2,1,0:T(8,128)(2,1)S(1)}, u32[]{:S(2)}, u32[]{:S(2)}) collective-permute-start(bf16[4,16,4608]{2,1,0:T(8,128)(2,1)S(1)} %get-tuple-element.120.refs_2_), channel_id=1, source_target_pairs={{0,4},{1,5},{2,6},{3,7},{4,0},{5,1},{6,2},{7,3},{8,12},{9,13},{10,... | collective-permute-start | bytes 1769480 | tf_op jit(solution)/shard_map/ppermute | solution.py:112
  151.1 35.9 %collective-permute-start.37 = (bf16[4,16,4608]{2,1,0:T(8,128)(2,1)S(1)}, bf16[4,16,4608]{2,1,0:T(8,128)(2,1)S(1)}, u32[]{:S(2)}, u32[]{:S(2)}) collective-permute-start(bf16[4,16,4608]{2,1,0:T(8,128)(2,1)S(1)} %get-tuple-element.119.refs_3_), channel_id=1, source_target_pairs={{0,5},{1,4},{2,7},{3,6},{4,1},{5,0},{6,3},{7,2},{8,13},{9,12},{10,... | collective-permute-start | bytes 1769480 | tf_op jit(solution)/shard_map/ppermute | solution.py:112
  186.4 4.7 %collective-permute-start.30 = (bf16[4,256,512]{2,1,0:T(8,128)(2,1)}, bf16[4,256,512]{2,1,0:T(8,128)(2,1)S(1)}, u32[]{:S(2)}, u32[]{:S(2)}) collective-permute-start(bf16[4,256,512]{2,1,0:T(8,128)(2,1)} %get-tuple-element.91), channel_id=1, source_target_pairs={{0,2},{2,0},{4,6},{6,4},{8,10},{10,8},{12,14},{14,12},{16,18},{18,... | collective-permute-start | bytes 3145736 | tf_op jit(solution)/shard_map/ppermute | solution.py:105
  186.5 29.6 %collective-permute-start.29 = (bf16[4,256,512]{2,1,0:T(8,128)(2,1)}, bf16[4,256,512]{2,1,0:T(8,128)(2,1)}, u32[]{:S(2)}, u32[]{:S(2)}) collective-permute-start(bf16[4,256,512]{2,1,0:T(8,128)(2,1)} %get-tuple-element.89), channel_id=1, source_target_pairs={{0,2},{2,0},{4,6},{6,4},{8,10},{10,8},{12,14},{14,12},{16,18},{18,... | collective-permute-start | bytes 3145736 | tf_op jit(solution)/shard_map/ppermute | solution.py:105
  187.3 4.9 %copy-start.28 = (bf16[16,4608]{1,0:T(8,128)(2,1)}, bf16[16,4608]{1,0:T(8,128)(2,1)S(1)}, u32[]{:S(2)}) copy-start(bf16[16,4608]{1,0:T(8,128)(2,1)S(1)} %get-tuple-element.125.refs_4_) | copy-start | bytes 442372
  187.3 4.9 %copy-start.29 = (bf16[16,4608]{1,0:T(8,128)(2,1)}, bf16[16,4608]{1,0:T(8,128)(2,1)S(1)}, u32[]{:S(2)}) copy-start(bf16[16,4608]{1,0:T(8,128)(2,1)S(1)} %get-tuple-element.126.refs_3_) | copy-start | bytes 442372
  187.3 4.9 %copy-start.30 = (bf16[16,4608]{1,0:T(8,128)(2,1)}, bf16[16,4608]{1,0:T(8,128)(2,1)S(1)}, u32[]{:S(2)}) copy-start(bf16[16,4608]{1,0:T(8,128)(2,1)S(1)} %get-tuple-element.127.refs_2_) | copy-start | bytes 442372
  187.3 27.6 %collective-permute-start.45 = (bf16[16,4608]{1,0:T(8,128)(2,1)S(1)}, bf16[16,4608]{1,0:T(8,128)(2,1)S(1)}, u32[]{:S(2)}, u32[]{:S(2)}) collective-permute-start(bf16[16,4608]{1,0:T(8,128)(2,1)S(1)} %get-tuple-element.127.refs_2_), channel_id=1, source_target_pairs={{0,8},{2,10},{4,12},{6,14},{8,16},{10,18},{12,20},{14,22},{16,24},... | collective-permute-start | bytes 442376 | tf_op jit(solution)/shard_map/ppermute | solution.py:102
  187.8 27.1 %collective-permute-start.46 = (bf16[16,4608]{1,0:T(8,128)(2,1)S(1)}, bf16[16,4608]{1,0:T(8,128)(2,1)S(1)}, u32[]{:S(2)}, u32[]{:S(2)}) collective-permute-start(bf16[16,4608]{1,0:T(8,128)(2,1)S(1)} %get-tuple-element.126.refs_3_), channel_id=1, source_target_pairs={{0,16},{2,18},{4,20},{6,22},{8,24},{10,26},{12,28},{14,30},{16,0},... | collective-permute-start | bytes 442376 | tf_op jit(solution)/shard_map/ppermute | solution.py:102
  190.0 25.0 %collective-permute-start.47 = (bf16[16,4608]{1,0:T(8,128)(2,1)S(1)}, bf16[16,4608]{1,0:T(8,128)(2,1)S(1)}, u32[]{:S(2)}, u32[]{:S(2)}) collective-permute-start(bf16[16,4608]{1,0:T(8,128)(2,1)S(1)} %get-tuple-element.125.refs_4_), channel_id=1, source_target_pairs={{0,24},{2,26},{4,28},{6,30},{8,0},{10,2},{12,4},{14,6},{16,8},{18,... | collective-permute-start | bytes 442376 | tf_op jit(solution)/shard_map/ppermute | solution.py:102
  191.6 24.7 %collective-permute-start.31 = (bf16[4,256,512]{2,1,0:T(8,128)(2,1)S(1)}, bf16[4,256,512]{2,1,0:T(8,128)(2,1)}, u32[]{:S(2)}, u32[]{:S(2)}) collective-permute-start(bf16[4,256,512]{2,1,0:T(8,128)(2,1)S(1)} %add_convert_fusion.refs_1_), channel_id=1, source_target_pairs={{0,4},{2,6},{4,0},{6,2},{8,12},{10,14},{12,8},{14,10},{16,20},{18,... | collective-permute-start | bytes 3145736 | tf_op jit(solution)/shard_map/ppermute | solution.py:105
  192.6 23.7 %copy-start.9 = (bf16[4,256,512]{2,1,0:T(8,128)(2,1)S(1)}, bf16[4,256,512]{2,1,0:T(8,128)(2,1)}, u32[]{:S(2)}) copy-start(bf16[4,256,512]{2,1,0:T(8,128)(2,1)} %get-tuple-element.88) | copy-start | bytes 3145732
  214.9 3.9 %collective-permute-start.38 = (bf16[4,4,16,1664]{3,2,1,0:T(8,128)(2,1)}, bf16[4,4,16,1664]{3,2,1,0:T(8,128)(2,1)S(1)}, u32[]{:S(2)}, u32[]{:S(2)}) collective-permute-start(bf16[4,4,16,1664]{3,2,1,0:T(8,128)(2,1)} %get-tuple-element.106), channel_id=1, source_target_pairs={{0,2},{2,0},{4,6},{6,4},{8,10},{10,8},{12,14},{14,12},{16,18},{18,... | collective-permute-start | bytes 2555912 | tf_op jit(solution)/shard_map/ppermute | solution.py:105
  219.7 8.2 %copy-start.8 = (bf16[256,512]{1,0:T(8,128)(2,1)S(1)}, bf16[256,512]{1,0:T(8,128)(2,1)}, u32[]{:S(2)}) copy-start(bf16[256,512]{1,0:T(8,128)(2,1)} %get-tuple-element.122.refs_1_) | copy-start | bytes 786436
  219.7 9.7 %copy-start.7 = (bf16[256,512]{1,0:T(8,128)(2,1)S(1)}, bf16[256,512]{1,0:T(8,128)(2,1)}, u32[]{:S(2)}) copy-start(bf16[256,512]{1,0:T(8,128)(2,1)} %get-tuple-element.124.refs_2_) | copy-start | bytes 786436
  219.7 10.4 %copy-start.6 = (bf16[256,512]{1,0:T(8,128)(2,1)S(1)}, bf16[256,512]{1,0:T(8,128)(2,1)}, u32[]{:S(2)}) copy-start(bf16[256,512]{1,0:T(8,128)(2,1)} %get-tuple-element.123.refs_3_) | copy-start | bytes 786436
  219.7 36.5 %copy-start.1 = (bf16[1,1024,512]{2,1,0:T(8,128)(2,1)S(1)}, bf16[1,1024,512]{2,1,0:T(8,128)(2,1)}, u32[]{:S(2)}) copy-start(bf16[1,1024,512]{2,1,0:T(8,128)(2,1)} %param.16) | copy-start | bytes 3145732
  222.3 7.8 %collective-permute-start.39 = (bf16[4,16,1664]{2,1,0:T(8,128)(2,1)}, bf16[4,16,1664]{2,1,0:T(8,128)(2,1)}, u32[]{:S(2)}, u32[]{:S(2)}) collective-permute-start(bf16[4,16,1664]{2,1,0:T(8,128)(2,1)} %get-tuple-element.131), channel_id=1, source_target_pairs={{0,1},{1,0},{2,3},{3,2},{4,5},{5,4},{6,7},{7,6},{8,9},{9,8},{10,11... | collective-permute-start | bytes 638984 | tf_op jit(solution)/shard_map/ppermute | solution.py:112
  222.8 9.0 %collective-permute-start.40 = (bf16[4,16,1664]{2,1,0:T(8,128)(2,1)}, bf16[4,16,1664]{2,1,0:T(8,128)(2,1)}, u32[]{:S(2)}, u32[]{:S(2)}) collective-permute-start(bf16[4,16,1664]{2,1,0:T(8,128)(2,1)} %get-tuple-element.130), channel_id=1, source_target_pairs={{0,4},{1,5},{2,6},{3,7},{4,0},{5,1},{6,2},{7,3},{8,12},{9,13},{10,... | collective-permute-start | bytes 638984 | tf_op jit(solution)/shard_map/ppermute | solution.py:112
  223.7 12.1 %collective-permute-start.41 = (bf16[4,16,1664]{2,1,0:T(8,128)(2,1)}, bf16[4,16,1664]{2,1,0:T(8,128)(2,1)}, u32[]{:S(2)}, u32[]{:S(2)}) collective-permute-start(bf16[4,16,1664]{2,1,0:T(8,128)(2,1)} %get-tuple-element.129), channel_id=1, source_target_pairs={{0,5},{1,4},{2,7},{3,6},{4,1},{5,0},{6,3},{7,2},{8,13},{9,12},{10,... | collective-permute-start | bytes 638984 | tf_op jit(solution)/shard_map/ppermute | solution.py:112
  227.2 30.4 %copy-start.21 = (f32[256,512]{1,0:T(8,128)S(1)}, f32[256,512]{1,0:T(8,128)}, u32[]{:S(2)}) copy-start(f32[256,512]{1,0:T(8,128)} %get-tuple-element.79) | copy-start | bytes 1572868
  227.9 11.2 %collective-permute-start.32 = (bf16[256,512]{1,0:T(8,128)(2,1)S(1)}, bf16[256,512]{1,0:T(8,128)(2,1)S(1)}, u32[]{:S(2)}, u32[]{:S(2)}) collective-permute-start(bf16[256,512]{1,0:T(8,128)(2,1)S(1)} %copy-done.8), channel_id=1, source_target_pairs={{0,24},{2,26},{4,28},{6,30},{8,0},{10,2},{12,4},{14,6},{16,8},{18,... | collective-permute-start | bytes 786440 | tf_op jit(solution)/shard_map/ppermute | solution.py:102
  229.5 26.7 %collective-permute-start.33 = (bf16[256,512]{1,0:T(8,128)(2,1)S(1)}, bf16[256,512]{1,0:T(8,128)(2,1)S(1)}, u32[]{:S(2)}, u32[]{:S(2)}) collective-permute-start(bf16[256,512]{1,0:T(8,128)(2,1)S(1)} %copy-done.7), channel_id=1, source_target_pairs={{0,16},{2,18},{4,20},{6,22},{8,24},{10,26},{12,28},{14,30},{16,0},... | collective-permute-start | bytes 786440 | tf_op jit(solution)/shard_map/ppermute | solution.py:102
  230.1 26.1 %collective-permute-start.34 = (bf16[256,512]{1,0:T(8,128)(2,1)S(1)}, bf16[256,512]{1,0:T(8,128)(2,1)S(1)}, u32[]{:S(2)}, u32[]{:S(2)}) collective-permute-start(bf16[256,512]{1,0:T(8,128)(2,1)S(1)} %copy-done.6), channel_id=1, source_target_pairs={{0,8},{2,10},{4,12},{6,14},{8,16},{10,18},{12,20},{14,22},{16,24},... | collective-permute-start | bytes 786440 | tf_op jit(solution)/shard_map/ppermute | solution.py:102
  236.9 20.9 %copy-start.12 = (bf16[768,512]{1,0:T(8,128)(2,1)S(1)}, bf16[768,512]{1,0:T(8,128)(2,1)}, u32[]{:S(2)}) copy-start(bf16[768,512]{1,0:T(8,128)(2,1)} %get-tuple-element.104) | copy-start | bytes 2359300
  237.0 22.0 %collective-permute-start.42 = (bf16[16,1664]{1,0:T(8,128)(2,1)S(1)}, bf16[16,1664]{1,0:T(8,128)(2,1)S(1)}, u32[]{:S(2)}, u32[]{:S(2)}) collective-permute-start(bf16[16,1664]{1,0:T(8,128)(2,1)S(1)} %get-tuple-element.132), channel_id=1, source_target_pairs={{0,8},{2,10},{4,12},{6,14},{8,16},{10,18},{12,20},{14,22},{16,24},... | collective-permute-start | bytes 159752 | tf_op jit(solution)/shard_map/ppermute | solution.py:102
  237.8 21.1 %collective-permute-start.43 = (bf16[16,1664]{1,0:T(8,128)(2,1)S(1)}, bf16[16,1664]{1,0:T(8,128)(2,1)S(1)}, u32[]{:S(2)}, u32[]{:S(2)}) collective-permute-start(bf16[16,1664]{1,0:T(8,128)(2,1)S(1)} %get-tuple-element.134), channel_id=1, source_target_pairs={{0,16},{2,18},{4,20},{6,22},{8,24},{10,26},{12,28},{14,30},{16,0},... | collective-permute-start | bytes 159752 | tf_op jit(solution)/shard_map/ppermute | solution.py:102
  239.1 19.8 %collective-permute-start.44 = (bf16[16,1664]{1,0:T(8,128)(2,1)S(1)}, bf16[16,1664]{1,0:T(8,128)(2,1)S(1)}, u32[]{:S(2)}, u32[]{:S(2)}) collective-permute-start(bf16[16,1664]{1,0:T(8,128)(2,1)S(1)} %get-tuple-element.133), channel_id=1, source_target_pairs={{0,24},{2,26},{4,28},{6,30},{8,0},{10,2},{12,4},{14,6},{16,8},{18,... | collective-permute-start | bytes 159752 | tf_op jit(solution)/shard_map/ppermute | solution.py:102
  (32 other events, 47.1 us)
